TPU v7x, 256 devices: a whole 4x4x8 slice. The times are simulated.
256 devices in a mesh: lat: 16 (over y_hi, z), lon: 4 (over y_lo, core), dp: 4 (over x).
Axes of the slice: x: 4, y: 4 (y_hi: 2, y_lo: 2; y = y_hi * 2 + y_lo), z: 8, core: 2. Of those that a mesh axis runs over, the one named last changes fastest.
Arguments:
- inputs: bfloat16 [4, 4, 192, 24, 1024], P('dp', None, 'lat', 'lon'), may hold values from -8 to 8
- cotangent: bfloat16 [4, 4, 192, 24, 1024], P('dp', None, 'lat', 'lon'), may hold values from -6 to 6
- gain: float32 [1024], replicated, may hold values from 0.1 to 1.9
- w_qkv: bfloat16 [1024, 1536], replicated, may hold values from -0.125 to 0.125
- w_proj: bfloat16 [512, 1024], replicated, may hold values from -0.25 to 0.25
- window_ids: int32 [4, 192, 24], P(None, 'lat', 'lon'), may hold values from 0 to 3, as said below
Outputs:
- outputs: bfloat16 [4, 4, 192, 24, 1024], P('dp', None, 'lat', 'lon')
- input_grad: bfloat16 [4, 4, 192, 24, 1024], P('dp', None, 'lat', 'lon')
- qkv_grad: float32 [1024, 1536], P(('lat', 'lon', 'dp'))
- proj_grad: float32 [512, 1024], P(None, ('lat', 'lon', 'dp'))
- gain_grad: float32 [1024], P(('lat', 'lon', 'dp'))
Inputs may be any that keep to these rules, and one draw needn't show every extreme that they name: `window_ids`: inside each window of the shifted grid the labels are equal over levels and form four rectangles cut by one latitude row and one longitude column, labelled 0 to 3.
All inputs are finite; a program needn't handle non-finite values.
Results may differ from a plain program's by a relative error of at most 0.014.
The roundings to bfloat16 on the way count: a program that leaves them out, or rounds other values in their place, can miss the bound.
Values may be sent and summed in bfloat16 or wider, within the bound.
A program may use at most 128 MiB of HBM per device.

v0:
```python
import math

import jax
import jax.numpy as jnp
from jax import lax
from jax.sharding import PartitionSpec as P

HEADS = 8
HSZ = 64
WL = 2
WA = 12
WO = 6


def from_behind(block, axis, distance):
    devices = range(lax.axis_size(axis))
    route = [((i - distance) % len(devices), i) for i in devices]
    return lax.ppermute(block, axis, route)


def to_windows(array):
    dims = array.shape
    array = array.reshape(dims[0], dims[1] // WL, WL, dims[2] // WA, WA, dims[3] // WO, WO, dims[4])
    array = array.transpose(0, 1, 3, 5, 2, 4, 6, 7)
    return array.reshape(-1, WL * WA * WO, dims[4])


def from_windows(windowed, grid_shape):
    array = windowed.reshape(
        grid_shape[0],
        grid_shape[1] // WL,
        grid_shape[2] // WA,
        grid_shape[3] // WO,
        WL,
        WA,
        WO,
        grid_shape[4],
    )
    return array.transpose(0, 1, 4, 2, 5, 3, 6, 7).reshape(grid_shape)


def forward_strips(stacked):
    half_a = WA // 2
    half_o = WO // 2
    upper_strip = from_behind(stacked[..., :half_a, :, :], "lat", -1)
    stacked = jnp.concatenate((stacked[..., half_a:, :, :], upper_strip), axis=stacked.ndim - 3)
    side_strip = from_behind(stacked[..., :half_o, :], "lon", -1)
    return jnp.concatenate((stacked[..., half_o:, :], side_strip), axis=stacked.ndim - 2)


def back_strips(stacked):
    half_a = WA // 2
    half_o = WO // 2
    rows_n = stacked.shape[-3]
    cols_n = stacked.shape[-2]
    lower_strip = from_behind(stacked[..., rows_n - half_a :, :, :], "lat", 1)
    stacked = jnp.concatenate(
        (lower_strip, stacked[..., : rows_n - half_a, :, :]), axis=stacked.ndim - 3
    )
    side_strip = from_behind(stacked[..., cols_n - half_o :, :], "lon", 1)
    return jnp.concatenate((side_strip, stacked[..., : cols_n - half_o, :]), axis=stacked.ndim - 2)


def window_core(queries, key_rows, values, same_group, d_out):
    score_scale = queries.shape[-1] ** (-0.5)
    scores = (
        jnp.einsum("gqhe,gkhe->ghqk", queries, key_rows, preferred_element_type=jnp.float32)
        * score_scale
    )
    scores = jnp.where(same_group[:, None], scores, -1e30)
    scores = scores - jnp.max(scores, axis=-1, keepdims=True)
    exp_scores = jnp.exp(scores)
    attn_prob = exp_scores / jnp.sum(exp_scores, axis=-1, keepdims=True)
    prob_half = attn_prob.astype(jnp.bfloat16)
    attended = jnp.einsum(
        "ghqk,gkhe->gqhe", prob_half, values, preferred_element_type=jnp.float32
    ).astype(jnp.bfloat16)
    d_prob = jnp.einsum("gqhe,gkhe->ghqk", d_out, values, preferred_element_type=jnp.float32)
    d_values = jnp.einsum(
        "ghqk,gqhe->gkhe", prob_half, d_out, preferred_element_type=jnp.float32
    ).astype(jnp.bfloat16)
    d_scores = (
        attn_prob * (d_prob - jnp.sum(attn_prob * d_prob, axis=-1, keepdims=True)) * score_scale
    ).astype(jnp.bfloat16)
    d_queries = jnp.einsum(
        "ghqk,gkhe->gqhe", d_scores, key_rows, preferred_element_type=jnp.float32
    ).astype(jnp.bfloat16)
    d_keys = jnp.einsum(
        "ghqk,gqhe->gkhe", d_scores, queries, preferred_element_type=jnp.float32
    ).astype(jnp.bfloat16)
    return (attended, d_queries, d_keys, d_values)


def block_terms(x_win, dy_win, gain, w_qkv, w_proj, same_group):
    windows_n, span, width = x_win.shape
    x_flat = x_win.reshape(-1, width).astype(jnp.float32)
    token_mean = jnp.mean(x_flat, axis=-1, keepdims=True)
    centred = x_flat - token_mean
    inv_std = lax.rsqrt(jnp.mean(centred * centred, axis=-1, keepdims=True) + 1e-05)
    normed = centred * inv_std
    hidden = (normed * gain).astype(jnp.bfloat16)
    projected = jnp.dot(hidden, w_qkv, preferred_element_type=jnp.float32).astype(jnp.bfloat16)
    projected = projected.reshape(windows_n, span, 3, HEADS, HSZ)
    dy_flat = dy_win.reshape(-1, width)
    d_attended = jnp.dot(dy_flat, w_proj.T, preferred_element_type=jnp.float32).astype(jnp.bfloat16)
    d_attended = d_attended.reshape(windows_n, span, HEADS, HSZ)
    attended, d_q, d_k, d_v = window_core(
        projected[:, :, 0], projected[:, :, 1], projected[:, :, 2], same_group, d_attended
    )
    att_flat = attended.reshape(-1, HEADS * HSZ)
    y_flat = (x_flat + jnp.dot(att_flat, w_proj, preferred_element_type=jnp.float32)).astype(
        jnp.bfloat16
    )
    proj_term = jnp.dot(att_flat.T, dy_flat, preferred_element_type=jnp.float32)
    d_qkv = jnp.stack((d_q, d_k, d_v), axis=2).reshape(-1, 3 * HEADS * HSZ)
    qkv_term = jnp.dot(hidden.T, d_qkv, preferred_element_type=jnp.float32)
    d_hidden = jnp.dot(d_qkv, w_qkv.T, preferred_element_type=jnp.float32)
    gain_term = jnp.sum(d_hidden * normed, axis=0)
    d_normed = d_hidden * gain
    correction = (
        d_normed
        - jnp.mean(d_normed, axis=-1, keepdims=True)
        - normed * jnp.mean(d_normed * normed, axis=-1, keepdims=True)
    )
    dx_flat = (dy_flat.astype(jnp.float32) + inv_std * correction).astype(jnp.bfloat16)
    return (y_flat, dx_flat, qkv_term, proj_term, gain_term)


def on_device(inputs, cotangent, gain, w_qkv, w_proj, window_ids):
    shifted = forward_strips(jnp.stack((inputs, cotangent)))
    grid_shape = inputs.shape
    x_win = to_windows(shifted[0])
    dy_win = to_windows(shifted[1])
    ids_win = to_windows(window_ids[None, :, :, :, None])[:, :, 0]
    same_group = ids_win[:, :, None] == ids_win[:, None, :]
    y_flat, dx_flat, qkv_term, proj_term, gain_term = block_terms(
        x_win, dy_win, gain, w_qkv, w_proj, same_group
    )
    ys = from_windows(y_flat, grid_shape)
    dxs = from_windows(dx_flat, grid_shape)
    outputs = back_strips(ys[None])[0]
    input_grad = back_strips(dxs[None])[0]
    n_lat = lax.axis_size("lat")
    n_lon = lax.axis_size("lon")
    n_rep = lax.axis_size("dp")
    cells = grid_shape[0] * grid_shape[1] * grid_shape[2] * grid_shape[3] * n_lat * n_lon * n_rep
    scale_back = 1.0 / math.sqrt(cells)
    summed = (
        lax.psum_scatter(qkv_term, ("lat", "lon", "dp"), scatter_dimension=0, tiled=True),
        lax.psum_scatter(proj_term, ("lat", "lon", "dp"), scatter_dimension=1, tiled=True),
        lax.psum_scatter(gain_term, ("lat", "lon", "dp"), scatter_dimension=0, tiled=True),
    )
    qkv_part = summed[0]
    proj_part = summed[1]
    gain_part = summed[2]
    return (
        outputs,
        input_grad,
        qkv_part * scale_back,
        proj_part * scale_back,
        gain_part * scale_back,
    )


def solution(mesh):
    return jax.shard_map(
        on_device,
        mesh=mesh,
        in_specs=(
            P("dp", None, "lat", "lon", None),
            P("dp", None, "lat", "lon", None),
            P(),
            P(),
            P(),
            P(None, "lat", "lon"),
        ),
        out_specs=(
            P("dp", None, "lat", "lon", None),
            P("dp", None, "lat", "lon", None),
            P(("lat", "lon", "dp"), None),
            P(None, ("lat", "lon", "dp")),
            P(("lat", "lon", "dp")),
        ),
        check_vma=False,
    )
```

profile of v0, /device:TPU:1, one launch (start us, length us, event | category | flops | bytes accessed | tf_op | source)
XLA Modules:
  0.0 417.3 jit_solution(11799322490267011894)
XLA Ops:
  9.5 9.1 %collective-permute-start = (bf16[2,1,4,6,6,1024]{5,2,4,3,1,0:T(4,128)(2,1)S(1)}, bf16[2,1,4,6,6,1024]{5,2,4,3,1,0:T(4,128)(2,1)S(1)}, u32[]{:S(2)}, u32[]{:S(2)}) collective-permute-start(bf16[2,1,4,6,6,1024]{5,2,4,3,1,0:T(4,128)(2,1)S(1)} %get-tuple-element.28), channel_id=1, source_target_pairs={{16,0},{32,16},{48,32},{64,48},{80,64},{96,80},{112,96},{128,112},... | collective-permute-start | bytes 1769480 | tf_op jit(solution)/shard_map/ppermute | solution.py:18
  18.6 12.0 %collective-permute-done = bf16[2,1,4,6,6,1024]{5,2,4,3,1,0:T(4,128)(2,1)S(1)} collective-permute-done((bf16[2,1,4,6,6,1024]{5,2,4,3,1,0:T(4,128)(2,1)S(1)}, bf16[2,1,4,6,6,1024]{5,2,4,3,1,0:T(4,128)(2,1)S(1)}, u32[]{:S(2)}, u32[]{:S(2)}) %collective-permute-start) | collective-permute-done | bytes 589856 | tf_op jit(solution)/shard_map/ppermute | solution.py:18
  34.9 7.2 %collective-permute-done.1 = bf16[2,1,4,12,3,1024]{5,2,4,3,1,0:T(4,128)(2,1)} collective-permute-done((bf16[2,1,4,12,3,1024]{5,2,4,3,1,0:T(4,128)(2,1)}, bf16[2,1,4,12,3,1024]{5,2,4,3,1,0:T(4,128)(2,1)}, u32[]{:S(2)}, u32[]{:S(2)}) %collective-permute-start.1) | collective-permute-done | bytes 589856 | tf_op jit(solution)/shard_map/ppermute | solution.py:18
  46.1 2.5 copy.45
  58.9 2.4 multiply_convert_fusion.1
  61.3 2.5 reshape.96
  63.8 3.4 convolution_convert_fusion
  67.2 3.5 reshape.92
  70.6 2.7 fusion.73
  80.0 3.6 fusion.76
  83.6 3.3 fusion.20
  90.0 5.6 %fusion.24 = bf16[2,144,1,8,64]{1,4,3,0,2:T(8,128)(2,1)} fusion(f32[2,8,144,144]{2,3,1,0:T(8,128)} %fusion.49, bf16[2,144,1,8,64]{1,4,3,0,2:T(8,128)(2,1)} %copy.70, f32[2,8,144,144]{2,3,1,0:T(8,128)} %get-tuple-element.34, f32[2,8,144]{2,1,0:T(8,128)S(1)} %get-tuple-element.33), kind=kOutput, calls=%fused_computation.21 | convolution fusion | flops 44939664 | bytes 3253248 | tf_op jit(solution)/shard_map/ghqk,gkhe->gqhe/dot_general | solution.py:85
  95.6 5.6 %fusion.21 = bf16[2,144,1,8,64]{1,4,3,0,2:T(8,128)(2,1)} fusion(f32[2,8,144,144]{2,3,1,0:T(8,128)} %fusion.49, bf16[2,144,1,8,64]{1,4,3,0,2:T(8,128)(2,1)} %copy.69, f32[2,8,144,144]{2,3,1,0:T(8,128)} %get-tuple-element.34, f32[2,8,144]{2,1,0:T(8,128)S(1)} %get-tuple-element.33), kind=kOutput, calls=%fused_computation.20 | convolution fusion | flops 44939664 | bytes 3253248 | tf_op jit(solution)/shard_map/ghqk,gqhe->gkhe/dot_general | solution.py:88
  109.1 2.9 pad_maximum_fusion
  111.9 3.9 copy.60
  115.8 3.6 reshape.95
  119.4 3.3 fusion.82
  122.7 4.5 %fusion.81 = f32[1024,1536]{1,0:T(8,128)} fusion(bf16[288,1024]{1,0:T(8,128)(2,1)S(1)} %copy-done.6, bf16[288,1536]{1,0:T(8,128)(2,1)S(1)} %copy-done.3), kind=kOutput, calls=%fused_computation.93 | convolution fusion | flops 905969664 | bytes 7766016 | tf_op jit(solution)/shard_map/dot_general | solution.py:116
  127.2 2.9 fusion.12
  134.2 2.6 multiply_reduce_fusion.1
  141.5 12.3 %collective-permute-done.2 = bf16[1,1,4,6,6,1024]{5,4,3,2,1,0:T(8,128)(2,1)} collective-permute-done((bf16[1,1,4,6,6,1024]{5,4,3,2,1,0:T(8,128)(2,1)}, bf16[1,1,4,6,6,1024]{5,4,3,2,1,0:T(8,128)(2,1)}, u32[]{:S(2)}, u32[]{:S(2)}) %collective-permute-start.2) | collective-permute-done | bytes 294944 | tf_op jit(solution)/shard_map/ppermute | solution.py:18
  156.0 9.4 %collective-permute-done.4 = bf16[1,1,4,6,6,1024]{5,4,3,2,1,0:T(8,128)(2,1)S(1)} collective-permute-done((bf16[1,1,4,6,6,1024]{5,4,3,2,1,0:T(8,128)(2,1)S(1)}, bf16[1,1,4,6,6,1024]{5,4,3,2,1,0:T(8,128)(2,1)S(1)}, u32[]{:S(2)}, u32[]{:S(2)}) %collective-permute-start.4) | collective-permute-done | bytes 294944 | tf_op jit(solution)/shard_map/ppermute | solution.py:18
  166.5 75.3 %all-reduce.2 = f32[1024]{0:T(1024)S(1)} all-reduce(f32[1024]{0:T(1024)S(1)} %get-tuple-element.15), channel_id=4, replica_groups=mesh['lat'=16,'lon'=4,'dp'=4] {'lat','lon','dp'}, use_global_device_ids=true, to_apply=%region_10.11.clone | all-reduce | flops 1024 | bytes 8192
  247.9 159.9 %all-reduce.6.cloned.1.call-done = (f32[1024,1536]{1,0:T(8,128)}, f32[512,1024]{0,1:T(8,128)}) async-done(((f32[1024,1536]{1,0:T(8,128)}, f32[512,1024]{0,1:T(8,128)}), (f32[1024,1536]{1,0:T(8,128)}, f32[512,1024]{0,1:T(8,128)})) %all-reduce.6.cloned.1.call-update) | async-done | bytes 8388624
  (82 shorter events, 59.5 us)
Async XLA Ops:
  7.2 56.7 %copy-start = (bf16[1024,1536]{1,0:T(8,128)(2,1)S(1)}, bf16[1024,1536]{1,0:T(8,128)(2,1)}, u32[]{:S(2)}) copy-start(bf16[1024,1536]{1,0:T(8,128)(2,1)} %param.9) | copy-start | bytes 9437188
  7.2 400.6 %all-reduce.6.cloned.1.call-start = ((), (), s32[]{:S(2)}) async-start(), calls=%async_computation | async-start | bytes 16777216
  9.5 24.4 %copy-start.13 = (s32[4,12,6]{1,0,2:T(4,128)S(1)}, s32[4,12,6]{1,0,2:T(4,128)}, u32[]{:S(2)}) copy-start(s32[4,12,6]{1,0,2:T(4,128)} %param.11) | copy-start | bytes 3460
  9.5 21.1 %collective-permute-start = (bf16[2,1,4,6,6,1024]{5,2,4,3,1,0:T(4,128)(2,1)S(1)}, bf16[2,1,4,6,6,1024]{5,2,4,3,1,0:T(4,128)(2,1)S(1)}, u32[]{:S(2)}, u32[]{:S(2)}) collective-permute-start(bf16[2,1,4,6,6,1024]{5,2,4,3,1,0:T(4,128)(2,1)S(1)} %get-tuple-element.28), channel_id=1, source_target_pairs={{16,0},{32,16},{48,32},{64,48},{80,64},{96,80},{112,96},{128,112},... | collective-permute-start | bytes 1769480 | tf_op jit(solution)/shard_map/ppermute | solution.py:18
  32.4 9.7 %collective-permute-start.1 = (bf16[2,1,4,12,3,1024]{5,2,4,3,1,0:T(4,128)(2,1)}, bf16[2,1,4,12,3,1024]{5,2,4,3,1,0:T(4,128)(2,1)}, u32[]{:S(2)}, u32[]{:S(2)}) collective-permute-start(bf16[2,1,4,12,3,1024]{5,2,4,3,1,0:T(4,128)(2,1)} %get-tuple-element.26), channel_id=1, source_target_pairs={{4,0},{8,4},{12,8},{0,12},{5,1},{9,5},{13,9},{1,13},{6,2},{10,6},{... | collective-permute-start | bytes 1769480 | tf_op jit(solution)/shard_map/ppermute | solution.py:18
  53.7 5.3 %copy-start.12 = (f32[1024]{0:T(1024)S(1)}, f32[1024]{0:T(1024)}, u32[]{:S(2)}) copy-start(f32[1024]{0:T(1024)} %param.8) | copy-start | bytes 12292
  73.3 6.7 %copy-start.11 = (pred[2,144,144]{1,2,0:T(8,128)(4,1)S(1)}, pred[2,144,144]{1,2,0:T(8,128)(4,1)}, u32[]{:S(2)}) copy-start(pred[2,144,144]{1,2,0:T(8,128)(4,1)} %broadcast_compare_fusion) | copy-start | bytes 124420
  83.6 3.3 copy-start.8
  83.6 3.3 copy-start.14
  86.9 1.1 copy-start.7
  119.4 3.3 copy-start.3
  119.4 3.3 copy-start.6
  132.2 2.0 copy-start.1
  134.2 2.6 copy-start.2
  134.2 19.6 %collective-permute-start.2 = (bf16[1,1,4,6,6,1024]{5,4,3,2,1,0:T(8,128)(2,1)}, bf16[1,1,4,6,6,1024]{5,4,3,2,1,0:T(8,128)(2,1)}, u32[]{:S(2)}, u32[]{:S(2)}) collective-permute-start(bf16[1,1,4,6,6,1024]{5,4,3,2,1,0:T(8,128)(2,1)} %get-tuple-element.31), channel_id=1, source_target_pairs={{240,0},{0,16},{16,32},{32,48},{48,64},{64,80},{80,96},{96,112},{1... | collective-permute-start | bytes 884744 | tf_op jit(solution)/shard_map/ppermute | solution.py:18
  141.4 23.9 %copy-start.4 = (bf16[1,1,4,6,6,1024]{5,4,3,2,1,0:T(8,128)(2,1)}, bf16[1,1,4,6,6,1024]{5,4,3,2,1,0:T(8,128)(2,1)S(1)}, u32[]{:S(2)}) copy-start(bf16[1,1,4,6,6,1024]{5,4,3,2,1,0:T(8,128)(2,1)S(1)} %get-tuple-element.30) | copy-start | bytes 884740
  141.4 23.9 %collective-permute-start.4 = (bf16[1,1,4,6,6,1024]{5,4,3,2,1,0:T(8,128)(2,1)S(1)}, bf16[1,1,4,6,6,1024]{5,4,3,2,1,0:T(8,128)(2,1)S(1)}, u32[]{:S(2)}, u32[]{:S(2)}) collective-permute-start(bf16[1,1,4,6,6,1024]{5,4,3,2,1,0:T(8,128)(2,1)S(1)} %get-tuple-element.29), channel_id=1, source_target_pairs={{240,0},{0,16},{16,32},{32,48},{48,64},{64,80},{80,96},{96,112},{1... | collective-permute-start | bytes 884744 | tf_op jit(solution)/shard_map/ppermute | solution.py:18
  156.0 86.4 %collective-permute-start.3 = (bf16[1,1,4,12,3,1024]{5,4,3,2,1,0:T(4,128)(2,1)}, bf16[1,1,4,12,3,1024]{5,4,3,2,1,0:T(4,128)(2,1)}, u32[]{:S(2)}, u32[]{:S(2)}) collective-permute-start(bf16[1,1,4,12,3,1024]{5,4,3,2,1,0:T(4,128)(2,1)} %fusion.53), channel_id=1, source_target_pairs={{12,0},{0,4},{4,8},{8,12},{13,1},{1,5},{5,9},{9,13},{14,2},{2,6},{... | collective-permute-start | bytes 884744 | tf_op jit(solution)/shard_map/ppermute | solution.py:18
  165.4 1.1 copy-start.9
  166.5 78.7 %collective-permute-start.5 = (bf16[1,1,4,12,3,1024]{5,4,3,2,1,0:T(4,128)(2,1)}, bf16[1,1,4,12,3,1024]{5,4,3,2,1,0:T(4,128)(2,1)}, u32[]{:S(2)}, u32[]{:S(2)}) collective-permute-start(bf16[1,1,4,12,3,1024]{5,4,3,2,1,0:T(4,128)(2,1)} %fusion.52), channel_id=1, source_target_pairs={{12,0},{0,4},{4,8},{8,12},{13,1},{1,5},{5,9},{9,13},{14,2},{2,6},{... | collective-permute-start | bytes 884744 | tf_op jit(solution)/shard_map/ppermute | solution.py:18
  242.4 2.9 copy-start.5
  242.4 2.9 copy-start.10
Sparse Core Ops, SparseCore 0:
  127.3 280.4 all-reduce.5
where the time goes:
time: 419 us; the launch traced here: 417 us
  waiting for transfers between devices  201 us (48%)
  blocking collectives  75.3 us (18%)
  local copies, waits for them, and re-layouts  50.5 us (12%)
  matrix products  39.7 us (9%)
  other arithmetic  26.1 us (6%)
  between operations  14.2 us (3%)
  starting transfers between devices  10.8 us (3%)
    unnamed x2, waiting for transfers between devices  160 us
    unnamed x1, blocking collectives  75.3 us
    ppermute x6, waiting for transfers between devices, from_behind(): return lax.ppermute(block, axis, route)  40.9 us
    ppermute x6, starting transfers between devices, from_behind(): return lax.ppermute(block, axis, route)  10.8 us
    unnamed x36, local copies, waits for them, and re-layouts  9.39 us
  transfers between devices with their start and end apart: 7, of which 5 were waited for; matrix products, arithmetic and copies ran while one was open for 6% of the time, Pallas kernels for 0%

commit v1 on v0

v1 whole, which is shorter than its diff:
```python
import functools
import math

import jax
import jax.numpy as jnp
from jax import lax
from jax.experimental import pallas as pl
from jax.experimental.pallas import tpu as pltpu
from jax.sharding import PartitionSpec as P

HEADS = 8
HSZ = 64
WA = 12
WO = 6
HALF_A = WA // 2
HALF_O = WO // 2
LEV = 4
CELLS = WA * WO
ROWS = CELLS * LEV
SPAN = 2 * CELLS
D = 1024
QKV = 3 * HEADS * HSZ
ATT = HEADS * HSZ
COLS = QKV + ATT
MESH = pl.DeviceIdType.MESH
F32 = jnp.float32
BF16 = jnp.bfloat16


def place():
    return lax.axis_index("lat"), lax.axis_index("lon"), lax.axis_index("dp")


def wrap(value, size):
    return lax.rem(value + size, size)


def partners():
    lat, lon, dp = place()
    odd = lax.rem(lon, 2)
    turn = 2 * odd - 1
    to = [
        (wrap(lat + turn, 16), lon, dp),
        (lat, wrap(lon - 1, 4), dp),
        (wrap(lat - turn, 16), wrap(lon - 1, 4), dp),
    ]
    source = [
        (wrap(lat - turn, 16), lon, dp),
        (lat, wrap(lon + 1, 4), dp),
        (wrap(lat - turn, 16), wrap(lon + 1, 4), dp),
    ]
    sent = [(odd, 1), (odd, 0), (1 - odd, 0)]
    taken = [(odd, 1), (1 - odd, 0), (odd, 0)]
    own = (1 - odd, 1)
    return odd, to, source, sent, taken, own


def block_part(ref, part):
    return ref.at[pl.ds(part[0] * HALF_A, HALF_A), pl.ds(part[1] * HALF_O, HALF_O)]


def window_part(ref, part):
    return ref.at[pl.ds((1 - part[0]) * HALF_A, HALF_A), pl.ds((1 - part[1]) * HALF_O, HALF_O)]


def greet(devices, count):
    barrier = pltpu.get_barrier_semaphore()
    for device in devices:
        pl.semaphore_signal(barrier, inc=1, device_id=device, device_id_type=MESH)
    pl.semaphore_wait(barrier, count)


def remote(src, dst, send_sem, recv_sem, device):
    return pltpu.make_async_remote_copy(
        src_ref=src, dst_ref=dst, send_sem=send_sem, recv_sem=recv_sem, device_id=device, device_id_type=MESH
    )


def halo_kernel(x_ref, dy_ref, ids_ref, xw_ref, dyw_ref, idw_ref, send_sem, recv_sem, own_sem):
    odd, to, source, sent, taken, own = partners()
    greet(source, 3)
    copies = []
    for n, (src, dst) in enumerate(((x_ref, xw_ref), (dy_ref, dyw_ref))):
        for k in range(3):
            copies.append(
                remote(
                    block_part(src, sent[k]),
                    window_part(dst, sent[k]),
                    send_sem.at[3 * n + k],
                    recv_sem.at[3 * n + k],
                    to[k],
                )
            )
            copies[-1].start()
    local = [
        pltpu.make_async_copy(block_part(x_ref, own), window_part(xw_ref, own), own_sem.at[0]),
        pltpu.make_async_copy(block_part(dy_ref, own), window_part(dyw_ref, own), own_sem.at[1]),
    ]
    for copy in local:
        copy.start()

    @pl.when(odd == 1)
    def _():
        labels = remote(ids_ref, idw_ref, send_sem.at[6], recv_sem.at[6], to[0])
        labels.start()
        labels.wait()

    @pl.when(odd == 0)
    def _():
        labels = pltpu.make_async_copy(ids_ref, idw_ref, own_sem.at[2])
        labels.start()
        labels.wait()

    for copy in copies + local:
        copy.wait()


def halo(x, dy, ids):
    block = jax.ShapeDtypeStruct((WA, WO, LEV, D), BF16)
    return pl.pallas_call(
        halo_kernel,
        out_shape=(block, block, jax.ShapeDtypeStruct(ids.shape, ids.dtype)),
        in_specs=[pl.BlockSpec(memory_space=pl.ANY)] * 3,
        out_specs=(pl.BlockSpec(memory_space=pl.ANY),) * 3,
        scratch_shapes=[
            pltpu.SemaphoreType.DMA((7,)),
            pltpu.SemaphoreType.DMA((7,)),
            pltpu.SemaphoreType.DMA((3,)),
        ],
        compiler_params=pltpu.CompilerParams(collective_id=1, has_side_effects=True),
        name="halo_in",
    )(x, dy, ids)


def dot(a, b):
    return jnp.dot(a, b, preferred_element_type=F32)


def dot_nt(a, b):
    return lax.dot_general(a, b, (((1,), (1,)), ((), ())), preferred_element_type=F32)


def dot_tn(a, b):
    return lax.dot_general(a, b, (((0,), (0,)), ((), ())), preferred_element_type=F32)


def spread(block_ref, wide):
    def step(c, _):
        pair = jnp.concatenate((block_ref[2 * c].astype(F32), block_ref[2 * c + 1].astype(F32)), axis=0)
        for j in range(D // 128):
            wide[j, pl.ds(pl.multiple_of(8 * c, 8), 8), :] = pair[:, 128 * j : 128 * j + 128]
        return 0

    lax.fori_loop(0, CELLS // 2, step, 0, unroll=4)


def gather(wide, block_ref):
    def step(c, _):
        pair = jnp.concatenate([wide[j, pl.ds(pl.multiple_of(8 * c, 8), 8), :] for j in range(D // 128)], axis=1)
        block_ref[2 * c] = pair[:LEV].astype(BF16)
        block_ref[2 * c + 1] = pair[LEV:].astype(BF16)
        return 0

    lax.fori_loop(0, CELLS // 2, step, 0, unroll=4)


def load_level(wide, level):
    return jnp.concatenate([wide[j, pl.ds(level, CELLS, stride=LEV), :] for j in range(D // 128)], axis=1)


def store_level(wide, level, value):
    for j in range(D // 128):
        wide[j, pl.ds(level, CELLS, stride=LEV), :] = value[:, 128 * j : 128 * j + 128]


def rows_of(level):
    return pl.ds(level * CELLS, CELLS)


def core_kernel(
    xw_ref,
    dyw_ref,
    lab_ref,
    gain_ref,
    wqkv_ref,
    wproj_ref,
    y_ref,
    dx_ref,
    g_ref,
    wide,
    xs,
    normed,
    inv,
    hid,
    dys,
    qkv,
    datt,
    att,
    dqkv,
    same,
):
    gain = gain_ref[...]
    spread(xw_ref, wide)
    for level in range(LEV):
        x = load_level(wide, level)
        centred = x - jnp.mean(x, axis=-1, keepdims=True)
        inv_std = lax.rsqrt(jnp.mean(centred * centred, axis=-1, keepdims=True) + 1e-05)
        unit = centred * inv_std
        xs[rows_of(level), :] = x
        normed[rows_of(level), :] = unit
        inv[rows_of(level), :] = jnp.broadcast_to(inv_std, (CELLS, 128))
        hid[rows_of(level), :] = (unit * gain).astype(BF16)
    spread(dyw_ref, wide)
    for level in range(LEV):
        dys[rows_of(level), :] = load_level(wide, level).astype(BF16)
    qkv[...] = dot(hid[...], wqkv_ref[...]).astype(BF16)
    datt[...] = dot_nt(dys[...], wproj_ref[...]).astype(BF16)
    for w in range(2):
        row = jnp.broadcast_to(lab_ref[w : w + 1, :], (128, 128))
        one = (row == row.T)[:CELLS, :CELLS].astype(F32)
        two = jnp.concatenate((one, one), axis=1)
        same[w] = jnp.concatenate((two, two), axis=0)

    low = lax.broadcasted_iota(jnp.int32, (1, 128), 1) < HSZ

    def heads(step, _):
        for w in range(2):
            rows = pl.ds(w * SPAN, SPAN)
            at = pl.multiple_of(step * 128, 128)
            q2 = qkv[rows, pl.ds(at, 128)]
            k2 = qkv[rows, pl.ds(ATT + at, 128)]
            v2 = qkv[rows, pl.ds(2 * ATT + at, 128)]
            o2 = datt[rows, pl.ds(at, 128)]
            apart = []
            for keep in (low, jnp.logical_not(low)):
                keep_w = jnp.broadcast_to(keep, (SPAN, 128))
                qh = jnp.where(keep_w, q2.astype(F32) * (HSZ**-0.5), 0.0).astype(BF16)
                oh = jnp.where(keep_w, o2.astype(F32), 0.0).astype(BF16)
                scores = jnp.where(same[w] > 0.5, dot_nt(k2, qh), -1e30)
                scores = scores - jnp.max(scores, axis=0, keepdims=True)
                weight = jnp.exp(scores)
                prob = weight * (1.0 / jnp.sum(weight, axis=0, keepdims=True))
                prob_b = prob.astype(BF16)
                d_prob = dot_nt(v2, oh)
                inner = jnp.sum(prob * d_prob, axis=0, keepdims=True)
                d_score = (prob * (d_prob - inner) * (HSZ**-0.5)).astype(BF16)
                apart.append((dot_tn(prob_b, v2), dot_tn(d_score, k2), dot(d_score, q2), dot(prob_b, o2)))
            both = [jnp.where(low, first, second).astype(BF16) for first, second in zip(*apart)]
            att[rows, pl.ds(at, 128)] = both[0]
            dqkv[rows, pl.ds(at, 128)] = both[1]
            dqkv[rows, pl.ds(ATT + at, 128)] = both[2]
            dqkv[rows, pl.ds(2 * ATT + at, 128)] = both[3]
        return 0

    lax.fori_loop(0, HEADS // 2, heads, 0)

    for level in range(LEV):
        store_level(wide, level, xs[rows_of(level), :] + dot(att[rows_of(level), :], wproj_ref[...]))
    gather(wide, y_ref)
    for level in range(LEV):
        g = dot_nt(dqkv[rows_of(level), :], wqkv_ref[...]) * gain
        unit = normed[rows_of(level), :]
        correction = g - jnp.mean(g, axis=-1, keepdims=True) - unit * jnp.mean(g * unit, axis=-1, keepdims=True)
        inv_std = inv[rows_of(level), 0:1]
        store_level(wide, level, dys[rows_of(level), :].astype(F32) + inv_std * correction)
    gather(wide, dx_ref)
    for block in range(D // 128):
        at = block * 128
        left = dot_tn(hid[:, at : at + 128], dqkv[...]).astype(BF16)
        right = dot_tn(dys[:, at : at + 128], att[...]).astype(BF16)
        g_ref[pl.ds(8 * block, 8), :, 0:QKV] = left.reshape(8, 16, QKV)
        g_ref[pl.ds(8 * block, 8), :, QKV:COLS] = right.reshape(8, 16, ATT)


def core(xw, dyw, labels, gain, w_qkv, w_proj):
    block = jax.ShapeDtypeStruct((CELLS, LEV, D), BF16)
    vmem = pl.BlockSpec(memory_space=pltpu.VMEM)
    return pl.pallas_call(
        core_kernel,
        out_shape=(block, block, jax.ShapeDtypeStruct((64, 16, COLS), BF16)),
        in_specs=[vmem] * 6,
        out_specs=(vmem,) * 3,
        scratch_shapes=[
            pltpu.VMEM((D // 128, ROWS, 128), F32),
            pltpu.VMEM((ROWS, D), F32),
            pltpu.VMEM((ROWS, D), F32),
            pltpu.VMEM((ROWS, 128), F32),
            pltpu.VMEM((ROWS, D), BF16),
            pltpu.VMEM((ROWS, D), BF16),
            pltpu.VMEM((ROWS, QKV), BF16),
            pltpu.VMEM((ROWS, ATT), BF16),
            pltpu.VMEM((ROWS, ATT), BF16),
            pltpu.VMEM((ROWS, QKV), BF16),
            pltpu.VMEM((2, SPAN, SPAN), F32),
        ],
        compiler_params=pltpu.CompilerParams(vmem_limit_bytes=48 * 2**20),
        name="window_core",
    )(xw, dyw, labels, gain, w_qkv, w_proj)


def send_all(list_of):
    for copy in list_of:
        copy.start()
    return list_of


def wait_all(list_of):
    for copy in list_of:
        copy.wait()


def tail_kernel(
    yw_ref,
    dxw_ref,
    g_ref,
    y_ref,
    dx_ref,
    out_ref,
    mine,
    r1,
    sa,
    sb,
    ra,
    rb,
    ta,
    tb,
    r3a,
    r3b,
    u,
    r4,
    halo_send,
    halo_recv,
    own_sem,
    pair_sem,
    send2,
    recv2,
    send3,
    recv3,
    send4,
    recv4,
):
    lat, lon, dp = place()
    y_hi, z = lat // 8, lax.rem(lat, 8)
    y_lo, chip_core = lon // 2, lax.rem(lon, 2)
    y_pos = 2 * y_hi + y_lo
    pair = (lat, y_lo * 2 + 1 - chip_core, dp)
    along_x = [(lat, lon, lax.rem(dp + k, 4)) for k in range(1, 4)]
    along_y = []
    for k in range(1, 4):
        other = lax.rem(y_pos + k, 4)
        along_y.append((other // 2, lax.rem(other, 2)))
    y_devices = [(hi * 8 + z, lo * 2 + chip_core, dp) for hi, lo in along_y]
    along_z = [lax.rem(z + k, 8) for k in range(1, 8)]
    z_devices = [(y_hi * 8 + other, lon, dp) for other in along_z]
    odd, to, source, sent, taken, own = partners()

    greet(to + [pair] + along_x + y_devices + z_devices, 3 + 1 + 3 + 3 + 7)

    first = remote(g_ref.at[:, :, 1 - chip_core], r1, pair_sem.at[0], pair_sem.at[1], pair)
    first.start()
    own_half = pltpu.make_async_copy(g_ref.at[:, :, chip_core], mine, pair_sem.at[2])
    own_half.start()
    back = []
    for n, (src, dst) in enumerate(((yw_ref, y_ref), (dxw_ref, dx_ref))):
        for k in range(3):
            back.append(
                remote(
                    window_part(src, taken[k]),
                    block_part(dst, taken[k]),
                    halo_send.at[3 * n + k],
                    halo_recv.at[3 * n + k],
                    source[k],
                )
            )
            back[-1].start()
    local = [
        pltpu.make_async_copy(window_part(yw_ref, own), block_part(y_ref, own), own_sem.at[0]),
        pltpu.make_async_copy(window_part(dxw_ref, own), block_part(dx_ref, own), own_sem.at[1]),
    ]
    send_all(local)
    own_half.wait()
    first.wait()

    half = COLS // 2

    def add_pair(n, _):
        i, j = n // 2, lax.rem(n, 2)
        total = mine[i, j].astype(F32) + r1[i, j].astype(F32)
        for k in range(4):
            sa[k, i, j] = total[4 * k : 4 * k + 4, :half].astype(BF16)
        sb[i // 8, lax.rem(i, 8), j] = total[:, half:].astype(BF16)
        return 0

    lax.fori_loop(0, 32, add_pair, 0)

    stage2 = []
    for k in range(3):
        stage2.append(remote(sa.at[along_x[k][2]], ra.at[k], send2.at[k], recv2.at[k], along_x[k]))
        hi, lo = along_y[k]
        stage2.append(remote(sb.at[hi, :, lo], rb.at[k], send2.at[3 + k], recv2.at[3 + k], y_devices[k]))
    send_all(stage2)
    wait_all(stage2)

    def add_x(n, _):
        i, j = n // 2, lax.rem(n, 2)
        total = sa[dp, i, j].astype(F32)
        for k in range(3):
            total = total + ra[k, i, j].astype(F32)
        ta[i // 8, lax.rem(i, 8), j] = total.astype(BF16)
        return 0

    lax.fori_loop(0, 32, add_x, 0)

    def add_y(i, _):
        total = sb[y_hi, i, y_lo].astype(F32)
        for k in range(3):
            total = total + rb[k, i].astype(F32)
        for k in range(4):
            tb[k, i] = total[4 * k : 4 * k + 4].astype(BF16)
        return 0

    lax.fori_loop(0, 8, add_y, 0)

    stage3 = []
    for k in range(3):
        hi, lo = along_y[k]
        stage3.append(remote(ta.at[hi, :, lo], r3a.at[k], send3.at[k], recv3.at[k], y_devices[k]))
        stage3.append(remote(tb.at[along_x[k][2]], r3b.at[k], send3.at[3 + k], recv3.at[3 + k], along_x[k]))
    send_all(stage3)
    wait_all(stage3)

    def add_last(i, _):
        left = ta[y_hi, i, y_lo].astype(F32)
        right = tb[dp, i].astype(F32)
        for k in range(3):
            left = left + r3a[k, i].astype(F32)
            right = right + r3b[k, i].astype(F32)
        u[i, :, 0:half] = left.astype(BF16)
        u[i, :, half:COLS] = right.astype(BF16)
        return 0

    lax.fori_loop(0, 8, add_last, 0)

    stage4 = []
    for k in range(7):
        stage4.append(remote(u.at[along_z[k]], r4.at[k], send4.at[k], recv4.at[k], z_devices[k]))
    send_all(stage4)
    wait_all(stage4)
    total = u[z].astype(F32)
    for k in range(7):
        total = total + r4[k].astype(F32)
    out_ref[...] = total * (1.0 / math.sqrt(73728))
    wait_all(back)
    wait_all(local)


def tail(yw, dxw, g):
    block = jax.ShapeDtypeStruct((WA, WO, LEV, D), BF16)
    half = COLS // 2
    any_space = pl.BlockSpec(memory_space=pl.ANY)
    dma = pltpu.SemaphoreType.DMA
    return pl.pallas_call(
        tail_kernel,
        out_shape=(block, block, jax.ShapeDtypeStruct((4, COLS), F32)),
        in_specs=[any_space] * 3,
        out_specs=(any_space, any_space, pl.BlockSpec(memory_space=pltpu.VMEM)),
        scratch_shapes=[
            pltpu.VMEM((16, 2, 16, COLS), BF16),
            pltpu.VMEM((16, 2, 16, COLS), BF16),
            pltpu.VMEM((4, 16, 2, 4, half), BF16),
            pltpu.VMEM((2, 8, 2, 16, half), BF16),
            pltpu.VMEM((3, 16, 2, 4, half), BF16),
            pltpu.VMEM((3, 8, 16, half), BF16),
            pltpu.VMEM((2, 8, 2, 4, half), BF16),
            pltpu.VMEM((4, 8, 4, half), BF16),
            pltpu.VMEM((3, 8, 4, half), BF16),
            pltpu.VMEM((3, 8, 4, half), BF16),
            pltpu.VMEM((8, 4, COLS), BF16),
            pltpu.VMEM((7, 4, COLS), BF16),
            dma((6,)),
            dma((6,)),
            dma((2,)),
            dma((3,)),
            dma((6,)),
            dma((6,)),
            dma((6,)),
            dma((6,)),
            dma((7,)),
            dma((7,)),
        ],
        compiler_params=pltpu.CompilerParams(
            collective_id=2, has_side_effects=True, vmem_limit_bytes=32 * 2**20
        ),
        name="halo_out_and_sum",
    )(yw, dxw, g)


def cells_first(block):
    return block.transpose(0, 2, 3, 1, 4).reshape(WA, WO, LEV, D)


def on_device(inputs, cotangent, gain, w_qkv, w_proj, window_ids):
    x = cells_first(inputs)
    dy = cells_first(cotangent)
    ids = jnp.stack((window_ids[0].reshape(CELLS), window_ids[2].reshape(CELLS)))
    ids = jnp.pad(ids, ((0, 6), (0, 128 - CELLS)))
    xw, dyw, idw = halo(x, dy, ids)
    flat = (CELLS, LEV, D)
    yw, dxw, g = core(xw.reshape(flat), dyw.reshape(flat), idw, gain.reshape(1, D), w_qkv, w_proj)
    grid = (WA, WO, LEV, D)
    y, dx, share = tail(yw.reshape(grid), dxw.reshape(grid), g.reshape(16, 2, 2, 16, COLS))
    lat, lon, dp = place()
    first_row = 4 * (lat * 16 + lon * 4 + dp)
    qkv_part = share[:, :QKV]
    proj_part = share[:, QKV:].T
    w_rows = lax.dynamic_slice(w_qkv, (first_row, 0), (4, QKV)).astype(F32)
    gain_part = jnp.sum(w_rows * qkv_part, axis=-1) / lax.dynamic_slice(gain, (first_row,), (4,))
    back = lambda block: block[None].transpose(0, 3, 1, 2, 4)
    return back(y), back(dx), qkv_part, proj_part, gain_part


def solution(mesh):
    return jax.shard_map(
        on_device,
        mesh=mesh,
        in_specs=(
            P("dp", None, "lat", "lon", None),
            P("dp", None, "lat", "lon", None),
            P(),
            P(),
            P(),
            P(None, "lat", "lon"),
        ),
        out_specs=(
            P("dp", None, "lat", "lon", None),
            P("dp", None, "lat", "lon", None),
            P(("lat", "lon", "dp"), None),
            P(None, ("lat", "lon", "dp")),
            P(("lat", "lon", "dp")),
        ),
        check_vma=False,
    )
```

time: 419 us -> 95.1 us (0.23)
  waiting for transfers between devices: 201 us -> 0 us
  Pallas kernels: 0 us -> 80.3 us
  blocking collectives: 75.3 us -> 0 us
  matrix products: 39.7 us -> 0 us
  local copies, waits for them, and re-layouts: 50.5 us -> 10.9 us
  other arithmetic: 26.1 us -> 2.75 us
  between operations: 14.2 us -> 0.69 us
  starting transfers between devices: 10.8 us -> 0 us
    unnamed x2 -> x0, waiting for transfers between devices: 160 us -> none
    pallas_call x0 -> x3, Pallas kernels: none -> 80.3 us  [the longest x1 40.5 us: tail(): pl.pallas_call(tail_kernel, out_shape=(block, block, jax.ShapeDtypeStruct...]
    unnamed x1 -> x0, blocking collectives: 75.3 us -> none
    ppermute x6 -> x0, waiting for transfers between devices: 40.9 us -> none  [from_behind(): return lax.ppermute(block, axis, route)]
    dot_general x11 -> x0, matrix products: 36.1 us -> none  [the longest x1 5.61 us: window_core(): jnp.einsum('ghqk,gkhe->gqhe', d_scores, key_rows, preferred_element_type=...]
    reshape x5 -> x0, local copies, waits for them, and re-layouts: 11.9 us -> none  [the longest x1 3.63 us: block_terms(): d_qkv = jnp.stack((d_q, d_k, d_v), axis=2).reshape(-1, 3 * HEADS * HSZ)]
    convert_element_type x5 -> x0, local copies, waits for them, and re-layouts: 11.4 us -> none  [the longest x2 4.96 us: block_terms(): x_flat = x_win.reshape(-1, width).astype(jnp.float32)]
    ppermute x6 -> x0, starting transfers between devices: 10.8 us -> none  [from_behind(): return lax.ppermute(block, axis, route)]
  transfers between devices with their start and end apart: 7 -> 0, of which waited for: 5 -> 0; matrix products, arithmetic and copies ran while one was open for 6% -> 0% of each run, Pallas kernels for 0% -> 0%
where the time goes in v1:
time: 95.1 us; the launch traced here: 94.6 us
  Pallas kernels  80.3 us (84%)
  local copies, waits for them, and re-layouts  10.9 us (11%)
  other arithmetic  2.75 us (3%)
    pallas_call x1, Pallas kernels, tail(): pl.pallas_call(tail_kernel, out_shape=(block, block, jax.ShapeDtypeStruct...  40.5 us
    pallas_call x1, Pallas kernels, core(): pl.pallas_call(core_kernel, out_shape=(block, block, jax.ShapeDtypeStruct...  20 us
    pallas_call x1, Pallas kernels, halo(): pl.pallas_call(halo_kernel, out_shape=(block, block, jax.ShapeDtypeStruct...  19.8 us
    unnamed x14, local copies, waits for them, and re-layouts  8.52 us

profile of v1, /device:TPU:1, one launch (start us, length us, event | category | flops | bytes accessed | tf_op | source)
XLA Modules:
  0.0 94.6 jit_solution(11314812270046962172)
XLA Ops:
  0.6 0.8 fusion
  1.4 0.1 copy.13
  1.5 0.1 stack_reshape_squeeze.6
  1.6 0.1 copy.14
  1.7 0.1 stack_reshape_squeeze.7
  1.8 0.6 pad.4.ids_ref
  2.4 19.8 %halo_in.1 = (bf16[12,6,4,1024]{3,2,1,0:T(4,128)(2,1)}, bf16[12,6,4,1024]{3,2,1,0:T(4,128)(2,1)}, s32[8,128]{1,0:T(8,128)}) custom-call(bf16[12,6,4,1024]{3,2,1,0:T(4,128)(2,1)} %bitcast.28, bf16[12,6,4,1024]{3,2,1,0:T(4,128)(2,1)} %bitcast.29, s32[8,128]{1,0:T(8,128)} %pad.4.ids_ref), custom_call_target="tpu_custom_call" | custom-call | tf_op jit(solution)/shard_map/halo_in/pallas_call | solution.py:120
  22.2 0.0 copy-start.1
  22.2 1.2 %copy-done.1 = bf16[512,1024]{1,0:T(8,128)(2,1)S(1)} copy-done((bf16[512,1024]{1,0:T(8,128)(2,1)S(1)}, bf16[512,1024]{1,0:T(8,128)(2,1)}, u32[]{:S(2)}) %copy-start.1) | copy-done | bytes 1048600
  23.5 0.0 copy-start.2
  23.5 1.1 %copy-done.2 = bf16[12,6,4,1024]{3,2,1,0:T(4,128)(2,1)S(1)} copy-done((bf16[12,6,4,1024]{3,2,1,0:T(4,128)(2,1)S(1)}, bf16[12,6,4,1024]{3,2,1,0:T(4,128)(2,1)}, u32[]{:S(2)}) %copy-start.2) | copy-done | bytes 589848
  24.5 0.0 copy-start.3
  24.5 1.1 %copy-done.3 = bf16[12,6,4,1024]{3,2,1,0:T(4,128)(2,1)S(1)} copy-done((bf16[12,6,4,1024]{3,2,1,0:T(4,128)(2,1)S(1)}, bf16[12,6,4,1024]{3,2,1,0:T(4,128)(2,1)}, u32[]{:S(2)}) %copy-start.3) | copy-done | bytes 589848
  25.6 0.0 copy-start.4
  25.6 0.7 copy-done.4
  26.3 0.7 copy-done.5
  26.9 20.0 %window_core.1 = (bf16[72,4,1024]{2,1,0:T(4,128)(2,1)S(1)}, bf16[72,4,1024]{2,1,0:T(4,128)(2,1)S(1)}, bf16[64,16,2048]{2,1,0:T(8,128)(2,1)}) custom-call(bf16[72,4,1024]{2,1,0:T(4,128)(2,1)S(1)} %bitcast.25, bf16[72,4,1024]{2,1,0:T(4,128)(2,1)S(1)} %bitcast.26, s32[8,128]{1,0:T(8,128)S(1)} %copy-done.5, f32[1,1024]{1,0:T(1,128)S(1)} %bitcast.27, ...), custom_call_target="tpu_custom_call" | custom-call | tf_op jit(solution)/shard_map/window_core/pallas_call | solution.py:278
  46.9 2.2 %copy-done = bf16[64,16,2048]{2,1,0:T(8,128)(2,1)S(1)} copy-done((bf16[64,16,2048]{2,1,0:T(8,128)(2,1)S(1)}, bf16[64,16,2048]{2,1,0:T(8,128)(2,1)}, u32[]{:S(2)}) %copy-start) | copy-done | bytes 4194328
  49.1 40.5 %halo_out_and_sum.1 = (bf16[12,6,4,1024]{3,2,1,0:T(4,128)(2,1)S(1)}, bf16[12,6,4,1024]{3,2,1,0:T(4,128)(2,1)S(1)}, f32[4,2048]{1,0:T(4,128)S(1)}) custom-call(bf16[12,6,4,1024]{3,2,1,0:T(4,128)(2,1)S(1)} %bitcast.23, bf16[12,6,4,1024]{3,2,1,0:T(4,128)(2,1)S(1)} %bitcast.24, bf16[16,2,2,16,2048]{4,3,2,1,0:T(8,128)(2,1)S(1)} %bitcast.20), custom_call_target="tpu_custom_call" | custom-call | tf_op jit(solution)/shard_map/halo_out_and_sum/pallas_call | solution.py:462
  89.6 1.5 %multiply_reduce_fusion = (f32[4]{0:T(128)S(1)}, f32[4,1536]{1,0:T(4,128)}) fusion(bf16[1024,1536]{1,0:T(8,128)(2,1)} %wqkv_ref.1, s32[]{:T(128)S(6)} %select_n.4, f32[4,2048]{1,0:T(4,128)S(1)} %get-tuple-element.22), kind=kLoop, calls=%fused_computation | loop fusion | flops 18428 | bytes 61460 | tf_op jit(solution)/shard_map/reduce_sum | solution.py:517
  91.1 1.3 %dynamic-slice_divide_fusion = f32[4]{0:T(128)} fusion(f32[4]{0:T(128)S(1)} %get-tuple-element.23, f32[1024]{0:T(1024)} %param.8, s32[]{:T(128)S(6)} %select_n.4), kind=kLoop, calls=%fused_computation.3 | loop fusion | flops 4 | bytes 52 | tf_op jit(solution)/shard_map/div | solution.py:517
  92.4 0.6 slice_bitcast_fusion
  93.0 0.8 copy.17
  93.8 0.8 copy.18
  (3 shorter events, 0.0 us)
Async XLA Ops:
  22.2 1.2 %copy-start.1 = (bf16[512,1024]{1,0:T(8,128)(2,1)S(1)}, bf16[512,1024]{1,0:T(8,128)(2,1)}, u32[]{:S(2)}) copy-start(bf16[512,1024]{1,0:T(8,128)(2,1)} %wproj_ref.1) | copy-start | bytes 3145732
  23.5 1.1 %copy-start.2 = (bf16[12,6,4,1024]{3,2,1,0:T(4,128)(2,1)S(1)}, bf16[12,6,4,1024]{3,2,1,0:T(4,128)(2,1)}, u32[]{:S(2)}) copy-start(bf16[12,6,4,1024]{3,2,1,0:T(4,128)(2,1)} %get-tuple-element.14) | copy-start | bytes 1769476
  24.5 1.1 %copy-start.3 = (bf16[12,6,4,1024]{3,2,1,0:T(4,128)(2,1)S(1)}, bf16[12,6,4,1024]{3,2,1,0:T(4,128)(2,1)}, u32[]{:S(2)}) copy-start(bf16[12,6,4,1024]{3,2,1,0:T(4,128)(2,1)} %get-tuple-element.15) | copy-start | bytes 1769476
  25.6 0.7 copy-start.4
  26.3 0.7 copy-start.5
  46.9 2.2 %copy-start = (bf16[64,16,2048]{2,1,0:T(8,128)(2,1)S(1)}, bf16[64,16,2048]{2,1,0:T(8,128)(2,1)}, u32[]{:S(2)}) copy-start(bf16[64,16,2048]{2,1,0:T(8,128)(2,1)} %get-tuple-element.19) | copy-start | bytes 12582916

commit v2 on v0

v2 whole, which is shorter than its diff:
```python
import functools
import math

import jax
import jax.numpy as jnp
from jax import lax
from jax.experimental import pallas as pl
from jax.experimental.pallas import tpu as pltpu
from jax.sharding import PartitionSpec as P

HEADS = 8
HSZ = 64
WA = 12
WO = 6
HALF_A = WA // 2
HALF_O = WO // 2
LEV = 4
CELLS = WA * WO
ROWS = CELLS * LEV
SPAN = 2 * CELLS
D = 1024
QKV = 3 * HEADS * HSZ
ATT = HEADS * HSZ
COLS = QKV + ATT
CHUNKS = HEADS // 2
WIDE = COLS // CHUNKS
MESH = pl.DeviceIdType.MESH
F32 = jnp.float32
BF16 = jnp.bfloat16


def place():
    return lax.axis_index("lat"), lax.axis_index("lon"), lax.axis_index("dp")


def wrap(value, size):
    return lax.rem(value + size, size)


def partners():
    lat, lon, dp = place()
    odd = lax.rem(lon, 2)
    turn = 2 * odd - 1
    to = [
        (wrap(lat + turn, 16), lon, dp),
        (lat, wrap(lon - 1, 4), dp),
        (wrap(lat - turn, 16), wrap(lon - 1, 4), dp),
    ]
    source = [
        (wrap(lat - turn, 16), lon, dp),
        (lat, wrap(lon + 1, 4), dp),
        (wrap(lat - turn, 16), wrap(lon + 1, 4), dp),
    ]
    sent = [(odd, 1), (odd, 0), (1 - odd, 0)]
    taken = [(odd, 1), (1 - odd, 0), (odd, 0)]
    own = (1 - odd, 1)
    return odd, to, source, sent, taken, own


def block_part(ref, part):
    return ref.at[pl.ds(part[0] * HALF_A, HALF_A), pl.ds(part[1] * HALF_O, HALF_O)]


def window_part(ref, part):
    return ref.at[pl.ds((1 - part[0]) * HALF_A, HALF_A), pl.ds((1 - part[1]) * HALF_O, HALF_O)]


def remote(src, dst, send_sem, recv_sem, device):
    return pltpu.make_async_remote_copy(
        src_ref=src, dst_ref=dst, send_sem=send_sem, recv_sem=recv_sem, device_id=device, device_id_type=MESH
    )


def dot(a, b):
    return jnp.dot(a, b, preferred_element_type=F32)


def dot_nt(a, b):
    return lax.dot_general(a, b, (((1,), (1,)), ((), ())), preferred_element_type=F32)


def dot_tn(a, b):
    return lax.dot_general(a, b, (((0,), (0,)), ((), ())), preferred_element_type=F32)


def spread(block_ref, wide):
    def step(r, _):
        for c in range(WO // 2):
            pair = jnp.concatenate((block_ref[r, 2 * c].astype(F32), block_ref[r, 2 * c + 1].astype(F32)), axis=0)
            at = pl.multiple_of(24 * r + 8 * c, 8)
            for j in range(D // 128):
                wide[j, pl.ds(at, 8), :] = pair[:, 128 * j : 128 * j + 128]
        return 0

    lax.fori_loop(0, WA, step, 0, unroll=2)


def gather(wide, block_ref):
    def step(r, _):
        for c in range(WO // 2):
            at = pl.multiple_of(24 * r + 8 * c, 8)
            pair = jnp.concatenate([wide[j, pl.ds(at, 8), :] for j in range(D // 128)], axis=1)
            block_ref[r, 2 * c] = pair[:LEV].astype(BF16)
            block_ref[r, 2 * c + 1] = pair[LEV:].astype(BF16)
        return 0

    lax.fori_loop(0, WA, step, 0, unroll=2)


def load_level(wide, level):
    return jnp.concatenate([wide[j, pl.ds(level, CELLS, stride=LEV), :] for j in range(D // 128)], axis=1)


def store_level(wide, level, value):
    for j in range(D // 128):
        wide[j, pl.ds(level, CELLS, stride=LEV), :] = value[:, 128 * j : 128 * j + 128]


def rows_of(level):
    return pl.ds(level * CELLS, CELLS)


def window_masks(ids, same):
    labels = jnp.zeros((LEV, 128), F32)
    for c in range(WO):
        row = lax.broadcasted_iota(jnp.int32, (WA, 128), 0)
        cell = lax.broadcasted_iota(jnp.int32, (WA, 128), 1)
        place_of = jnp.where(cell == WO * row + c, 1.0, 0.0)
        labels = labels + dot(ids[c].astype(F32), place_of)
    for w in range(2):
        row = jnp.broadcast_to(labels[2 * w : 2 * w + 1, :], (128, 128))
        one = (row == row.T)[:CELLS, :CELLS].astype(F32)
        two = jnp.concatenate((one, one), axis=1)
        same[w] = jnp.concatenate((two, two), axis=0)


def head_pair(w, h, qkv, datt, same, att, dqkv):
    low = lax.broadcasted_iota(jnp.int32, (1, 128), 1) < HSZ
    rows = pl.ds(w * SPAN, SPAN)
    at = h * 128
    q2 = qkv[rows, pl.ds(at, 128)]
    k2 = qkv[rows, pl.ds(ATT + at, 128)]
    v2 = qkv[rows, pl.ds(2 * ATT + at, 128)]
    o2 = datt[rows, pl.ds(at, 128)]
    apart = []
    for keep in (low, jnp.logical_not(low)):
        keep_w = jnp.broadcast_to(keep, (SPAN, 128))
        qh = jnp.where(keep_w, q2.astype(F32) * (HSZ**-0.5), 0.0).astype(BF16)
        oh = jnp.where(keep_w, o2.astype(F32), 0.0).astype(BF16)
        scores = jnp.where(same[w] > 0.5, dot_nt(k2, qh), -1e30)
        scores = scores - jnp.max(scores, axis=0, keepdims=True)
        weight = jnp.exp(scores)
        prob = weight * (1.0 / jnp.sum(weight, axis=0, keepdims=True))
        prob_b = prob.astype(BF16)
        d_prob = dot_nt(v2, oh)
        inner = jnp.sum(prob * d_prob, axis=0, keepdims=True)
        d_score = (prob * (d_prob - inner) * (HSZ**-0.5)).astype(BF16)
        apart.append((dot_tn(prob_b, v2), dot_tn(d_score, k2), dot(d_score, q2), dot(prob_b, o2)))
    both = [jnp.where(low, first, second).astype(BF16) for first, second in zip(*apart)]
    att[rows, pl.ds(at, 128)] = both[0]
    dqkv[rows, pl.ds(at, 128)] = both[1]
    dqkv[rows, pl.ds(ATT + at, 128)] = both[2]
    dqkv[rows, pl.ds(2 * ATT + at, 128)] = both[3]


def core_kernel(
    x_ref,
    dy_ref,
    ids_ref,
    gain_ref,
    wqkv_ref,
    wproj_ref,
    y_ref,
    dx_ref,
    qkv_out,
    proj_out,
    gain_out,
    xin,
    dyin,
    xv,
    dyv,
    ids,
    ids_in,
    gain_v,
    wqkv,
    wproj,
    wide,
    xs,
    normed,
    inv,
    hid,
    dys,
    hid_t,
    dys_t,
    qkv,
    datt,
    att,
    dqkv,
    same,
    gbuf,
    r1,
    sx,
    sy,
    r2x,
    r2y,
    tx,
    ty,
    r3,
    u,
    r4,
    load_sem,
    in_send,
    in_recv,
    halo_send,
    halo_recv,
    own_sem,
    send1,
    recv1,
    send2,
    recv2,
    send3,
    recv3,
    send4,
    recv4,
):
    loads = [
        pltpu.make_async_copy(src, dst, load_sem.at[n])
        for n, (src, dst) in enumerate(
            (
                (x_ref, xin),
                (dy_ref, dyin),
                (gain_ref, gain_v),
                (ids_ref, ids_in),
                (wqkv_ref, wqkv),
                (wproj_ref, wproj),
            )
        )
    ]
    for copy in loads:
        copy.start()

    lat, lon, dp = place()
    y_hi, z = lat // 8, lax.rem(lat, 8)
    y_lo, chip_core = lon // 2, lax.rem(lon, 2)
    y_pos = 2 * y_hi + y_lo
    pair = (lat, y_lo * 2 + 1 - chip_core, dp)
    along_x = [lax.rem(dp + k, 4) for k in range(1, 4)]
    x_devices = [(lat, lon, other) for other in along_x]
    along_y = []
    for k in range(1, 4):
        other = lax.rem(y_pos + k, 4)
        along_y.append((other // 2, lax.rem(other, 2)))
    y_devices = [(hi * 8 + z, lo * 2 + chip_core, dp) for hi, lo in along_y]
    along_z = [lax.rem(z + k, 8) for k in range(1, 8)]
    z_devices = [(y_hi * 8 + other, lon, dp) for other in along_z]
    odd, to, source, sent, taken, own = partners()
    barrier = pltpu.get_barrier_semaphore()
    for device in to + source + [pair] + x_devices + y_devices + z_devices:
        pl.semaphore_signal(barrier, inc=1, device_id=device, device_id_type=MESH)

    for n in (0, 1, 3):
        loads[n].wait()
    pl.semaphore_wait(barrier, 3 + 3 + 1 + 3 + 3 + 7)
    arriving = [[], []]
    for n, (src, dst) in enumerate(((xin, xv), (dyin, dyv))):
        for k in range(3):
            sems = (in_send.at[3 * n + k], in_recv.at[3 * n + k])
            arriving[n].append(remote(block_part(src, sent[k]), window_part(dst, sent[k]), *sems, to[k]))
        arriving[n].append(pltpu.make_async_copy(block_part(src, own), window_part(dst, own), own_sem.at[n]))
        send_all(arriving[n])

    @pl.when(odd == 1)
    def _():
        labels = remote(ids_in, ids, in_send.at[6], in_recv.at[6], to[0])
        labels.start()
        labels.wait()

    @pl.when(odd == 0)
    def _():
        labels = pltpu.make_async_copy(ids_in, ids, own_sem.at[2])
        labels.start()
        labels.wait()

    window_masks(ids, same)
    loads[2].wait()
    wait_all(arriving[0])
    gain = gain_v[...]
    spread(xv, wide)
    for level in range(LEV):
        x = load_level(wide, level)
        centred = x - jnp.mean(x, axis=-1, keepdims=True)
        inv_std = lax.rsqrt(jnp.mean(centred * centred, axis=-1, keepdims=True) + 1e-05)
        unit = centred * inv_std
        xs[rows_of(level), :] = x
        normed[rows_of(level), :] = unit
        inv[rows_of(level), :] = jnp.broadcast_to(inv_std, (CELLS, 128))
        hid[rows_of(level), :] = (unit * gain).astype(BF16)
    wait_all(arriving[1])
    spread(dyv, wide)
    for level in range(LEV):
        dys[rows_of(level), :] = load_level(wide, level).astype(BF16)
    loads[4].wait()
    qkv[...] = dot(hid[...], wqkv[...]).astype(BF16)
    loads[5].wait()
    datt[...] = dot_nt(dys[...], wproj[...]).astype(BF16)
    hid_t[...] = hid[...].T
    dys_t[...] = dys[...].T

    def attend(h):
        for w in range(2):
            head_pair(w, h, qkv, datt, same, att, dqkv)

    def grad_chunk(h):
        at = h * 128
        left = jnp.concatenate([dqkv[:, n * ATT + at : n * ATT + at + 128] for n in range(3)], axis=1)
        right = att[:, at : at + 128]

        for n in range(2):
            rows = pl.ds(512 * n, 512)
            part = jnp.concatenate((dot(hid_t[rows, :], left), dot(dys_t[rows, :], right)), axis=1)
            gbuf[h, 8 * n : 8 * n + 8] = part.astype(BF16).reshape(8, 2, 2, 16, WIDE)

    def send_pair(h):
        copy = remote(gbuf.at[h, :, :, 1 - chip_core], r1.at[h], send1.at[h], recv1.at[h], pair)
        copy.start()
        return [copy]

    def add_pair(h):
        s = h // 2

        def step(n, _):
            i, j = n // 2, lax.rem(n, 2)
            total = gbuf[h, i, j, chip_core].astype(F32) + r1[h, i, j].astype(F32)
            if h % 2 == 0:
                for k in range(4):
                    sx[s, k, i // 8, lax.rem(i, 8), j] = total[4 * k : 4 * k + 4].astype(BF16)
            else:
                sy[s, i // 8, lax.rem(i, 8), j] = total.astype(BF16)
            return 0

        lax.fori_loop(0, 32, step, 0, unroll=2)
        copies = []
        for k in range(3):
            sems = (send2.at[h, k], recv2.at[h, k])
            if h % 2 == 0:
                copies.append(remote(sx.at[s, along_x[k]], r2x.at[s, k], *sems, x_devices[k]))
            else:
                hi, lo = along_y[k]
                copies.append(remote(sy.at[s, hi, :, lo], r2y.at[s, k], *sems, y_devices[k]))
        return send_all(copies)

    def add_second(h):
        s = h // 2
        if h % 2 == 0:

            def step(n, _):
                hi, i, j = n // 16, lax.rem(n // 2, 8), lax.rem(n, 2)
                total = sx[s, dp, hi, i, j].astype(F32)
                for k in range(3):
                    total = total + r2x[s, k, hi, i, j].astype(F32)
                tx[s, hi, i, j] = total.astype(BF16)
                return 0

            lax.fori_loop(0, 32, step, 0, unroll=2)
        else:

            def step(i, _):
                total = sy[s, y_hi, i, y_lo].astype(F32)
                for k in range(3):
                    total = total + r2y[s, k, i].astype(F32)
                for k in range(4):
                    ty[s, k, i] = total[4 * k : 4 * k + 4].astype(BF16)
                return 0

            lax.fori_loop(0, 8, step, 0, unroll=2)
        copies = []
        for k in range(3):
            sems = (send3.at[h, k], recv3.at[h, k])
            if h % 2 == 0:
                hi, lo = along_y[k]
                copies.append(remote(tx.at[s, hi, :, lo], r3.at[h, k], *sems, y_devices[k]))
            else:
                copies.append(remote(ty.at[s, along_x[k]], r3.at[h, k], *sems, x_devices[k]))
        return send_all(copies)

    def add_third(h):
        s = h // 2

        def step(i, _):
            total = (tx[s, y_hi, i, y_lo] if h % 2 == 0 else ty[s, dp, i]).astype(F32)
            for k in range(3):
                total = total + r3[h, k, i].astype(F32)
            u[i, :, WIDE * h : WIDE * h + WIDE] = total.astype(BF16)
            return 0

        lax.fori_loop(0, 8, step, 0, unroll=2)

    def send_last():
        return send_all(
            [remote(u.at[along_z[k]], r4.at[k], send4.at[k], recv4.at[k], z_devices[k]) for k in range(7)]
        )

    def add_last():
        total = u[z].astype(F32)
        for k in range(7):
            total = total + r4[k].astype(F32)
        total = total * (1.0 / math.sqrt(73728))
        for h in range(CHUNKS):
            for n in range(3):
                at = WIDE * h + 128 * n
                qkv_out[:, n * ATT + 128 * h : n * ATT + 128 * h + 128] = total[:, at : at + 128]
            proj_out[:, 128 * h : 128 * h + 128] = total[:, WIDE * h + 384 : WIDE * h + 512]

    def send_back(n, src, dst):
        copies = [
            remote(
                window_part(src, taken[k]),
                block_part(dst, taken[k]),
                halo_send.at[3 * n + k],
                halo_recv.at[3 * n + k],
                source[k],
            )
            for k in range(3)
        ]
        copies.append(pltpu.make_async_copy(window_part(src, own), block_part(dst, own), own_sem.at[3 + n]))
        return send_all(copies)

    first, second, third = [None] * 4, [None] * 4, [None] * 4
    for h in range(CHUNKS):
        attend(h)
        grad_chunk(h)
        first[h] = send_pair(h)
        if h > 0:
            wait_all(first[h - 1])
            second[h - 1] = add_pair(h - 1)

    xs[...] += dot(att[...], wproj[...])
    wait_all(first[3])
    second[3] = add_pair(3)
    for level in range(LEV):
        store_level(wide, level, xs[rows_of(level), :])
    gather(wide, xv)
    back = send_back(0, xv, y_ref)
    xs[...] = dot_nt(dqkv[...], wqkv[...])
    for level in range(LEV):
        g = xs[rows_of(level), :] * gain
        unit = normed[rows_of(level), :]
        correction = g - jnp.mean(g, axis=-1, keepdims=True) - unit * jnp.mean(g * unit, axis=-1, keepdims=True)
        inv_std = inv[rows_of(level), 0:1]
        store_level(wide, level, dys[rows_of(level), :].astype(F32) + inv_std * correction)
    gather(wide, dyv)
    back += send_back(1, dyv, dx_ref)
    for h in range(CHUNKS):
        wait_all(second[h])
        third[h] = add_second(h)
    for h in range(CHUNKS):
        wait_all(third[h])
        add_third(h)
    fourth = send_last()
    wait_all(fourth)
    add_last()

    group = lat * 4 + lon
    block = wqkv[pl.ds(pl.multiple_of(16 * group, 16), 16), :].astype(F32)
    w_rows = jnp.zeros((4, QKV), F32)
    for k in range(4):
        w_rows = w_rows + jnp.where(dp == k, block[4 * k : 4 * k + 4], 0.0)
    summed = jnp.sum(w_rows * qkv_out[...], axis=-1, keepdims=True)
    lanes = lax.broadcasted_iota(jnp.int32, (4, 128), 1)
    rows = lax.broadcasted_iota(jnp.int32, (4, 128), 0)
    near = gain_v[:, pl.ds(pl.multiple_of(128 * (group // 8), 128), 128)]
    at = lax.rem(group, 8) * 16 + dp * 4
    gains = jnp.sum(jnp.where(lanes == at + rows, jnp.broadcast_to(near, (4, 128)), 0.0), axis=-1, keepdims=True)
    ratio = jnp.broadcast_to(summed / gains, (4, 128))
    gain_out[...] = jnp.sum(jnp.where(lanes == rows, ratio, 0.0), axis=0, keepdims=True)
    wait_all(back)


def send_all(copies):
    for copy in copies:
        copy.start()
    return copies


def wait_all(copies):
    for copy in copies:
        copy.wait()


def core(x, dy, ids, gain, w_qkv, w_proj):
    block = jax.ShapeDtypeStruct((WA, WO, LEV, D), BF16)
    any_space = pl.BlockSpec(memory_space=pl.ANY)
    vmem = pl.BlockSpec(memory_space=pltpu.VMEM)
    dma = pltpu.SemaphoreType.DMA
    return pl.pallas_call(
        core_kernel,
        out_shape=(
            block,
            block,
            jax.ShapeDtypeStruct((4, QKV), F32),
            jax.ShapeDtypeStruct((4, ATT), F32),
            jax.ShapeDtypeStruct((1, 128), F32),
        ),
        in_specs=[any_space] * 6,
        out_specs=(any_space, any_space, vmem, vmem, vmem),
        scratch_shapes=[
            pltpu.VMEM((WA, WO, LEV, D), BF16),
            pltpu.VMEM((WA, WO, LEV, D), BF16),
            pltpu.VMEM((WA, WO, LEV, D), BF16),
            pltpu.VMEM((WA, WO, LEV, D), BF16),
            pltpu.VMEM((WO, LEV, WA), jnp.int32),
            pltpu.VMEM((WO, LEV, WA), jnp.int32),
            pltpu.VMEM((1, D), F32),
            pltpu.VMEM((D, QKV), BF16),
            pltpu.VMEM((ATT, D), BF16),
            pltpu.VMEM((D // 128, ROWS, 128), F32),
            pltpu.VMEM((ROWS, D), F32),
            pltpu.VMEM((ROWS, D), F32),
            pltpu.VMEM((ROWS, 128), F32),
            pltpu.VMEM((ROWS, D), BF16),
            pltpu.VMEM((ROWS, D), BF16),
            pltpu.VMEM((D, ROWS), BF16),
            pltpu.VMEM((D, ROWS), BF16),
            pltpu.VMEM((ROWS, QKV), BF16),
            pltpu.VMEM((ROWS, ATT), BF16),
            pltpu.VMEM((ROWS, ATT), BF16),
            pltpu.VMEM((ROWS, QKV), BF16),
            pltpu.VMEM((2, SPAN, SPAN), F32),
            pltpu.VMEM((4, 16, 2, 2, 16, WIDE), BF16),
            pltpu.VMEM((4, 16, 2, 16, WIDE), BF16),
            pltpu.VMEM((2, 4, 2, 8, 2, 4, WIDE), BF16),
            pltpu.VMEM((2, 2, 8, 2, 16, WIDE), BF16),
            pltpu.VMEM((2, 3, 2, 8, 2, 4, WIDE), BF16),
            pltpu.VMEM((2, 3, 8, 16, WIDE), BF16),
            pltpu.VMEM((2, 2, 8, 2, 4, WIDE), BF16),
            pltpu.VMEM((2, 4, 8, 4, WIDE), BF16),
            pltpu.VMEM((4, 3, 8, 4, WIDE), BF16),
            pltpu.VMEM((8, 4, COLS), BF16),
            pltpu.VMEM((7, 4, COLS), BF16),
            dma((6,)),
            dma((7,)),
            dma((7,)),
            dma((6,)),
            dma((6,)),
            dma((5,)),
            dma((4,)),
            dma((4,)),
            dma((4, 3)),
            dma((4, 3)),
            dma((4, 3)),
            dma((4, 3)),
            dma((7,)),
            dma((7,)),
        ],
        compiler_params=pltpu.CompilerParams(
            collective_id=1, has_side_effects=True, vmem_limit_bytes=56 * 2**20
        ),
        name="window_attention",
    )(x, dy, ids, gain, w_qkv, w_proj)


def finish_kernel(*refs):
    arrays, results, held, (sems,) = refs[:5], refs[5:10], refs[10:15], refs[15:]
    taken = send_all([pltpu.make_async_copy(arrays[n], held[n], sems.at[n]) for n in range(5)])
    put = []
    for n in range(4):
        taken[n].wait()
        put += send_all([pltpu.make_async_copy(held[n], results[n], sems.at[5 + n])])
    taken[4].wait()
    results[4][...] = held[4][:, :4]
    wait_all(put)


def finish(*arrays):
    any_space = pl.BlockSpec(memory_space=pl.ANY)
    shapes = [jax.ShapeDtypeStruct(a.shape, a.dtype) for a in arrays[:4]] + [jax.ShapeDtypeStruct((1, 4), F32)]
    return pl.pallas_call(
        finish_kernel,
        out_shape=tuple(shapes),
        in_specs=[any_space] * 5,
        out_specs=(any_space,) * 4 + (pl.BlockSpec(memory_space=pltpu.VMEM),),
        scratch_shapes=[pltpu.VMEM(a.shape, a.dtype) for a in arrays] + [pltpu.SemaphoreType.DMA((9,))],
        compiler_params=pltpu.CompilerParams(vmem_limit_bytes=56 * 2**20),
        name="results",
    )(*arrays)


def cells_first(block):
    return block.transpose(0, 2, 3, 1, 4).reshape(WA, WO, LEV, D)


def on_device(inputs, cotangent, gain, w_qkv, w_proj, window_ids):
    y, dx, qkv_part, proj_part, gain_part = core(
        cells_first(inputs),
        cells_first(cotangent),
        window_ids.transpose(2, 0, 1),
        gain.reshape(1, D),
        w_qkv,
        w_proj,
    )
    y, dx, qkv_part, proj_part, gain_part = finish(y, dx, qkv_part, proj_part, gain_part)
    back = lambda block: block[None].transpose(0, 3, 1, 2, 4)
    return back(y), back(dx), qkv_part, proj_part.T, gain_part.reshape(4)


def solution(mesh):
    return jax.shard_map(
        on_device,
        mesh=mesh,
        in_specs=(
            P("dp", None, "lat", "lon", None),
            P("dp", None, "lat", "lon", None),
            P(),
            P(),
            P(),
            P(None, "lat", "lon"),
        ),
        out_specs=(
            P("dp", None, "lat", "lon", None),
            P("dp", None, "lat", "lon", None),
            P(("lat", "lon", "dp"), None),
            P(None, ("lat", "lon", "dp")),
            P(("lat", "lon", "dp")),
        ),
        check_vma=False,
    )
```

time: 419 us -> 66.9 us (0.16)
  waiting for transfers between devices: 201 us -> 0 us
  blocking collectives: 75.3 us -> 0 us
  Pallas kernels: 0 us -> 66.2 us
  local copies, waits for them, and re-layouts: 50.5 us -> 0 us
  matrix products: 39.7 us -> 0 us
  other arithmetic: 26.1 us -> 0 us
  between operations: 14.2 us -> 0.64 us
  starting transfers between devices: 10.8 us -> 0 us
    unnamed x2 -> x0, waiting for transfers between devices: 160 us -> none
    unnamed x1 -> x0, blocking collectives: 75.3 us -> none
    pallas_call x0 -> x2, Pallas kernels: none -> 66.2 us  [the longest x1 63.5 us: core(): pl.pallas_call(core_kernel, out_shape=(block, block, jax.ShapeDtypeStruct...]
    ppermute x6 -> x0, waiting for transfers between devices: 40.9 us -> none  [from_behind(): return lax.ppermute(block, axis, route)]
    dot_general x11 -> x0, matrix products: 36.1 us -> none  [the longest x1 5.61 us: window_core(): jnp.einsum('ghqk,gkhe->gqhe', d_scores, key_rows, preferred_element_type=...]
    reshape x5 -> x0, local copies, waits for them, and re-layouts: 11.9 us -> none  [the longest x1 3.63 us: block_terms(): d_qkv = jnp.stack((d_q, d_k, d_v), axis=2).reshape(-1, 3 * HEADS * HSZ)]
    convert_element_type x5 -> x0, local copies, waits for them, and re-layouts: 11.4 us -> none  [the longest x2 4.96 us: block_terms(): x_flat = x_win.reshape(-1, width).astype(jnp.float32)]
    ppermute x6 -> x0, starting transfers between devices: 10.8 us -> none  [from_behind(): return lax.ppermute(block, axis, route)]
  transfers between devices with their start and end apart: 7 -> 0, of which waited for: 5 -> 0; matrix products, arithmetic and copies ran while one was open for 6% -> 0% of each run, Pallas kernels for 0% -> 0%
where the time goes in v2:
time: 66.9 us; the launch traced here: 66.8 us
  Pallas kernels  66.2 us (99%)
    pallas_call x1, Pallas kernels, core(): pl.pallas_call(core_kernel, out_shape=(block, block, jax.ShapeDtypeStruct...  63.5 us
    pallas_call x1, Pallas kernels, finish(): pl.pallas_call(finish_kernel, out_shape=tuple(shapes), in_specs=[any_spac...  2.67 us

profile of v2, /device:TPU:1, one launch (start us, length us, event | category | flops | bytes accessed | tf_op | source)
XLA Modules:
  0.0 66.8 jit_solution(7389358156995876277)
XLA Ops:
  0.6 63.5 %window_attention.1 = (bf16[12,6,4,1024]{3,2,1,0:T(4,128)(2,1)}, bf16[12,6,4,1024]{3,2,1,0:T(4,128)(2,1)}, f32[4,1536]{1,0:T(4,128)}, f32[4,512]{1,0:T(4,128)}, f32[1,128]{1,0:T(1,128)}) custom-call(bf16[12,6,4,1024]{3,2,1,0:T(4,128)(2,1)} %bitcast.16, bf16[12,6,4,1024]{3,2,1,0:T(4,128)(2,1)} %bitcast.17, s32[6,4,12]{2,1,0:T(4,128)} %bitcast.18, ...), custom_call_target="tpu_custom_call" | custom-call | tf_op jit(solution)/shard_map/window_attention/pallas_call | solution.py:495
  64.2 2.7 %results.1 = (bf16[12,6,4,1024]{3,2,1,0:T(4,128)(2,1)}, bf16[12,6,4,1024]{3,2,1,0:T(4,128)(2,1)}, f32[4,1536]{1,0:T(4,128)}, f32[4,512]{1,0:T(4,128)}, f32[1,4]{1,0:T(1,128)}) custom-call(bf16[12,6,4,1024]{3,2,1,0:T(4,128)(2,1)} %get-tuple-element.15.refs_0_, bf16[12,6,4,1024]{3,2,1,0:T(4,128)(2,1)} %get-tuple-element.16.refs_1_, ...), custom_call_target="tpu_custom_call" | custom-call | tf_op jit(solution)/shard_map/results/pallas_call | solution.py:577

commit v3 on v2

--- a/solution.py
+++ b/solution.py
@@ -24,6 +24,8 @@
 COLS = QKV + ATT
 CHUNKS = HEADS // 2
 WIDE = COLS // CHUNKS
+FIRST_AXIS = 'xyxx'
+SLOT = [FIRST_AXIS[:h].count(FIRST_AXIS[h]) for h in range(CHUNKS)]
 MESH = pl.DeviceIdType.MESH
 F32 = jnp.float32
 BF16 = jnp.bfloat16
@@ -37,24 +39,21 @@
     return lax.rem(value + size, size)
 
 
+def later(lon):
+    return 1 - lax.rem(lon, 2)
+
+
 def partners():
     lat, lon, dp = place()
-    odd = lax.rem(lon, 2)
-    turn = 2 * odd - 1
-    to = [
-        (wrap(lat + turn, 16), lon, dp),
-        (lat, wrap(lon - 1, 4), dp),
-        (wrap(lat - turn, 16), wrap(lon - 1, 4), dp),
-    ]
-    source = [
-        (wrap(lat - turn, 16), lon, dp),
-        (lat, wrap(lon + 1, 4), dp),
-        (wrap(lat - turn, 16), wrap(lon + 1, 4), dp),
-    ]
-    sent = [(odd, 1), (odd, 0), (1 - odd, 0)]
-    taken = [(odd, 1), (1 - odd, 0), (odd, 0)]
-    own = (1 - odd, 1)
-    return odd, to, source, sent, taken, own
+    west, east = wrap(lon - 1, 4), wrap(lon + 1, 4)
+    here, there = later(lon), later(west)
+    to = [(wrap(lat + 2 * here - 1, 16), lon, dp), (lat, west, dp), (wrap(lat + 2 * there - 1, 16), west, dp)]
+    other = wrap(lat + 1 - 2 * here, 16)
+    source = [(other, lon, dp), (lat, east, dp), (other, east, dp)]
+    sent = [(here, 1), (1 - there, 0), (there, 0)]
+    taken = [(here, 1), (1 - here, 0), (here, 0)]
+    own = (1 - here, 1)
+    return here, to, source, sent, taken, own
 
 
 def block_part(ref, part):
@@ -130,8 +129,8 @@
     for w in range(2):
         row = jnp.broadcast_to(labels[2 * w : 2 * w + 1, :], (128, 128))
         one = (row == row.T)[:CELLS, :CELLS].astype(F32)
-        two = jnp.concatenate((one, one), axis=1)
-        same[w] = jnp.concatenate((two, two), axis=0)
+        four = jnp.concatenate((one, one, one, one), axis=1)
+        same[w] = jnp.concatenate((four, four), axis=0)
 
 
 def head_pair(w, h, qkv, datt, same, att, dqkv):
@@ -142,21 +141,30 @@
     k2 = qkv[rows, pl.ds(ATT + at, 128)]
     v2 = qkv[rows, pl.ds(2 * ATT + at, 128)]
     o2 = datt[rows, pl.ds(at, 128)]
-    apart = []
-    for keep in (low, jnp.logical_not(low)):
-        keep_w = jnp.broadcast_to(keep, (SPAN, 128))
-        qh = jnp.where(keep_w, q2.astype(F32) * (HSZ**-0.5), 0.0).astype(BF16)
-        oh = jnp.where(keep_w, o2.astype(F32), 0.0).astype(BF16)
-        scores = jnp.where(same[w] > 0.5, dot_nt(k2, qh), -1e30)
-        scores = scores - jnp.max(scores, axis=0, keepdims=True)
-        weight = jnp.exp(scores)
-        prob = weight * (1.0 / jnp.sum(weight, axis=0, keepdims=True))
-        prob_b = prob.astype(BF16)
-        d_prob = dot_nt(v2, oh)
-        inner = jnp.sum(prob * d_prob, axis=0, keepdims=True)
-        d_score = (prob * (d_prob - inner) * (HSZ**-0.5)).astype(BF16)
-        apart.append((dot_tn(prob_b, v2), dot_tn(d_score, k2), dot(d_score, q2), dot(prob_b, o2)))
-    both = [jnp.where(low, first, second).astype(BF16) for first, second in zip(*apart)]
+    low_w = jnp.broadcast_to(low, (SPAN, 128))
+
+    def split(x, scale=1.0):
+        x = x.astype(F32) * scale
+        return jnp.concatenate((jnp.where(low_w, x, 0.0), jnp.where(low_w, 0.0, x)), axis=0).astype(BF16)
+
+    q4 = split(q2)
+    o4 = split(o2)
+    scores = jnp.where(same[w] > 0.5, dot_nt(k2, split(q2, HSZ**-0.5)), -1e30)
+    scores = scores - jnp.max(scores, axis=0, keepdims=True)
+    weight = jnp.exp(scores)
+    prob = weight * (1.0 / jnp.sum(weight, axis=0, keepdims=True))
+    prob_b = prob.astype(BF16)
+    d_prob = dot_nt(v2, o4)
+    inner = jnp.sum(prob * d_prob, axis=0, keepdims=True)
+    d_score = (prob * (d_prob - inner) * (HSZ**-0.5)).astype(BF16)
+    two_att = dot_tn(prob_b, v2)
+    two_dq = dot_tn(d_score, k2)
+    both = [
+        jnp.where(low, two_att[:SPAN], two_att[SPAN:]).astype(BF16),
+        jnp.where(low, two_dq[:SPAN], two_dq[SPAN:]).astype(BF16),
+        dot(d_score, q4).astype(BF16),
+        dot(prob_b, o4).astype(BF16),
+    ]
     att[rows, pl.ds(at, 128)] = both[0]
     dqkv[rows, pl.ds(at, 128)] = both[1]
     dqkv[rows, pl.ds(ATT + at, 128)] = both[2]
@@ -326,23 +334,23 @@
         return [copy]
 
     def add_pair(h):
-        s = h // 2
+        s = SLOT[h]
 
         def step(n, _):
             i, j = n // 2, lax.rem(n, 2)
-            total = gbuf[h, i, j, chip_core].astype(F32) + r1[h, i, j].astype(F32)
-            if h % 2 == 0:
+            total = gbuf[h, i, j, chip_core] + r1[h, i, j]
+            if FIRST_AXIS[h] == 'x':
                 for k in range(4):
-                    sx[s, k, i // 8, lax.rem(i, 8), j] = total[4 * k : 4 * k + 4].astype(BF16)
+                    sx[s, k, i // 8, lax.rem(i, 8), j] = total[4 * k : 4 * k + 4]
             else:
-                sy[s, i // 8, lax.rem(i, 8), j] = total.astype(BF16)
+                sy[s, i // 8, lax.rem(i, 8), j] = total
             return 0
 
         lax.fori_loop(0, 32, step, 0, unroll=2)
         copies = []
         for k in range(3):
             sems = (send2.at[h, k], recv2.at[h, k])
-            if h % 2 == 0:
+            if FIRST_AXIS[h] == 'x':
                 copies.append(remote(sx.at[s, along_x[k]], r2x.at[s, k], *sems, x_devices[k]))
             else:
                 hi, lo = along_y[k]
@@ -350,8 +358,8 @@
         return send_all(copies)
 
     def add_second(h):
-        s = h // 2
-        if h % 2 == 0:
+        s = SLOT[h]
+        if FIRST_AXIS[h] == 'x':
 
             def step(n, _):
                 hi, i, j = n // 16, lax.rem(n // 2, 8), lax.rem(n, 2)
@@ -376,7 +384,7 @@
         copies = []
         for k in range(3):
             sems = (send3.at[h, k], recv3.at[h, k])
-            if h % 2 == 0:
+            if FIRST_AXIS[h] == 'x':
                 hi, lo = along_y[k]
                 copies.append(remote(tx.at[s, hi, :, lo], r3.at[h, k], *sems, y_devices[k]))
             else:
@@ -384,10 +392,10 @@
         return send_all(copies)
 
     def add_third(h):
-        s = h // 2
+        s = SLOT[h]
 
         def step(i, _):
-            total = (tx[s, y_hi, i, y_lo] if h % 2 == 0 else ty[s, dp, i]).astype(F32)
+            total = (tx[s, y_hi, i, y_lo] if FIRST_AXIS[h] == 'x' else ty[s, dp, i]).astype(F32)
             for k in range(3):
                 total = total + r3[h, k, i].astype(F32)
             u[i, :, WIDE * h : WIDE * h + WIDE] = total.astype(BF16)
@@ -428,11 +436,11 @@
     first, second, third = [None] * 4, [None] * 4, [None] * 4
     for h in range(CHUNKS):
         attend(h)
-        grad_chunk(h)
-        first[h] = send_pair(h)
         if h > 0:
             wait_all(first[h - 1])
             second[h - 1] = add_pair(h - 1)
+        grad_chunk(h)
+        first[h] = send_pair(h)
 
     xs[...] += dot(att[...], wproj[...])
     wait_all(first[3])
@@ -525,14 +533,14 @@
             pltpu.VMEM((ROWS, ATT), BF16),
             pltpu.VMEM((ROWS, ATT), BF16),
             pltpu.VMEM((ROWS, QKV), BF16),
-            pltpu.VMEM((2, SPAN, SPAN), F32),
+            pltpu.VMEM((2, SPAN, 2 * SPAN), F32),
             pltpu.VMEM((4, 16, 2, 2, 16, WIDE), BF16),
             pltpu.VMEM((4, 16, 2, 16, WIDE), BF16),
-            pltpu.VMEM((2, 4, 2, 8, 2, 4, WIDE), BF16),
+            pltpu.VMEM((3, 4, 2, 8, 2, 4, WIDE), BF16),
             pltpu.VMEM((2, 2, 8, 2, 16, WIDE), BF16),
-            pltpu.VMEM((2, 3, 2, 8, 2, 4, WIDE), BF16),
+            pltpu.VMEM((3, 3, 2, 8, 2, 4, WIDE), BF16),
             pltpu.VMEM((2, 3, 8, 16, WIDE), BF16),
-            pltpu.VMEM((2, 2, 8, 2, 4, WIDE), BF16),
+            pltpu.VMEM((3, 2, 8, 2, 4, WIDE), BF16),
             pltpu.VMEM((2, 4, 8, 4, WIDE), BF16),
             pltpu.VMEM((4, 3, 8, 4, WIDE), BF16),
             pltpu.VMEM((8, 4, COLS), BF16),

time: 66.9 us -> 61.9 us (0.925)
  Pallas kernels: 66.2 us -> 61.1 us
    pallas_call x1, Pallas kernels: 63.5 us -> 58.5 us  [core(): pl.pallas_call(core_kernel, out_shape=(block, block, jax.ShapeDtypeStruct...]
where the time goes in v3:
time: 61.9 us; the launch traced here: 61.8 us
  Pallas kernels  61.1 us (99%)
  between operations  0.64 us (1%)
    pallas_call x1, Pallas kernels, core(): pl.pallas_call(core_kernel, out_shape=(block, block, jax.ShapeDtypeStruct...  58.5 us
    pallas_call x1, Pallas kernels, finish(): pl.pallas_call(finish_kernel, out_shape=tuple(shapes), in_specs=[any_spac...  2.67 us

profile of v3, /device:TPU:1, one launch (start us, length us, event | category | flops | bytes accessed | tf_op | source)
XLA Modules:
  0.0 61.8 jit_solution(9916321992386349000)
XLA Ops:
  0.6 58.5 %window_attention.1 = (bf16[12,6,4,1024]{3,2,1,0:T(4,128)(2,1)}, bf16[12,6,4,1024]{3,2,1,0:T(4,128)(2,1)}, f32[4,1536]{1,0:T(4,128)}, f32[4,512]{1,0:T(4,128)}, f32[1,128]{1,0:T(1,128)}) custom-call(bf16[12,6,4,1024]{3,2,1,0:T(4,128)(2,1)} %bitcast.16, bf16[12,6,4,1024]{3,2,1,0:T(4,128)(2,1)} %bitcast.17, s32[6,4,12]{2,1,0:T(4,128)} %bitcast.18, ...), custom_call_target="tpu_custom_call" | custom-call | tf_op jit(solution)/shard_map/window_attention/pallas_call | solution.py:503
  59.1 2.7 %results.1 = (bf16[12,6,4,1024]{3,2,1,0:T(4,128)(2,1)}, bf16[12,6,4,1024]{3,2,1,0:T(4,128)(2,1)}, f32[4,1536]{1,0:T(4,128)}, f32[4,512]{1,0:T(4,128)}, f32[1,4]{1,0:T(1,128)}) custom-call(bf16[12,6,4,1024]{3,2,1,0:T(4,128)(2,1)} %get-tuple-element.15.refs_0_, bf16[12,6,4,1024]{3,2,1,0:T(4,128)(2,1)} %get-tuple-element.16.refs_1_, ...), custom_call_target="tpu_custom_call" | custom-call | tf_op jit(solution)/shard_map/results/pallas_call | solution.py:585

commit v4 on v3

--- a/solution.py
+++ b/solution.py
@@ -270,12 +270,13 @@
         loads[n].wait()
     pl.semaphore_wait(barrier, 3 + 3 + 1 + 3 + 3 + 7)
     arriving = [[], []]
+    local = []
     for n, (src, dst) in enumerate(((xin, xv), (dyin, dyv))):
         for k in range(3):
             sems = (in_send.at[3 * n + k], in_recv.at[3 * n + k])
             arriving[n].append(remote(block_part(src, sent[k]), window_part(dst, sent[k]), *sems, to[k]))
-        arriving[n].append(pltpu.make_async_copy(block_part(src, own), window_part(dst, own), own_sem.at[n]))
-        send_all(arriving[n])
+        local.append(pltpu.make_async_copy(block_part(src, own), window_part(dst, own), own_sem.at[n]))
+        send_all(arriving[n] + local[n:])
 
     @pl.when(odd == 1)
     def _():
@@ -291,7 +292,8 @@
 
     window_masks(ids, same)
     loads[2].wait()
-    wait_all(arriving[0])
+    take_all(arriving[0])
+    local[0].wait()
     gain = gain_v[...]
     spread(xv, wide)
     for level in range(LEV):
@@ -303,7 +305,8 @@
         normed[rows_of(level), :] = unit
         inv[rows_of(level), :] = jnp.broadcast_to(inv_std, (CELLS, 128))
         hid[rows_of(level), :] = (unit * gain).astype(BF16)
-    wait_all(arriving[1])
+    take_all(arriving[1])
+    local[1].wait()
     spread(dyv, wide)
     for level in range(LEV):
         dys[rows_of(level), :] = load_level(wide, level).astype(BF16)
@@ -346,7 +349,7 @@
                 sy[s, i // 8, lax.rem(i, 8), j] = total
             return 0
 
-        lax.fori_loop(0, 32, step, 0, unroll=2)
+        lax.fori_loop(0, 32, step, 0, unroll=8)
         copies = []
         for k in range(3):
             sems = (send2.at[h, k], recv2.at[h, k])
@@ -369,7 +372,7 @@
                 tx[s, hi, i, j] = total.astype(BF16)
                 return 0
 
-            lax.fori_loop(0, 32, step, 0, unroll=2)
+            lax.fori_loop(0, 32, step, 0, unroll=8)
         else:
 
             def step(i, _):
@@ -380,7 +383,7 @@
                     ty[s, k, i] = total[4 * k : 4 * k + 4].astype(BF16)
                 return 0
 
-            lax.fori_loop(0, 8, step, 0, unroll=2)
+            lax.fori_loop(0, 8, step, 0, unroll=4)
         copies = []
         for k in range(3):
             sems = (send3.at[h, k], recv3.at[h, k])
@@ -401,7 +404,7 @@
             u[i, :, WIDE * h : WIDE * h + WIDE] = total.astype(BF16)
             return 0
 
-        lax.fori_loop(0, 8, step, 0, unroll=2)
+        lax.fori_loop(0, 8, step, 0, unroll=4)
 
     def send_last():
         return send_all(
@@ -437,13 +440,13 @@
     for h in range(CHUNKS):
         attend(h)
         if h > 0:
-            wait_all(first[h - 1])
+            take_all(first[h - 1])
             second[h - 1] = add_pair(h - 1)
         grad_chunk(h)
         first[h] = send_pair(h)
 
     xs[...] += dot(att[...], wproj[...])
-    wait_all(first[3])
+    take_all(first[3])
     second[3] = add_pair(3)
     for level in range(LEV):
         store_level(wide, level, xs[rows_of(level), :])
@@ -459,28 +462,31 @@
     gather(wide, dyv)
     back += send_back(1, dyv, dx_ref)
     for h in range(CHUNKS):
-        wait_all(second[h])
+        take_all(second[h])
         third[h] = add_second(h)
     for h in range(CHUNKS):
-        wait_all(third[h])
+        take_all(third[h])
         add_third(h)
     fourth = send_last()
-    wait_all(fourth)
-    add_last()
-
     group = lat * 4 + lon
     block = wqkv[pl.ds(pl.multiple_of(16 * group, 16), 16), :].astype(F32)
     w_rows = jnp.zeros((4, QKV), F32)
     for k in range(4):
         w_rows = w_rows + jnp.where(dp == k, block[4 * k : 4 * k + 4], 0.0)
-    summed = jnp.sum(w_rows * qkv_out[...], axis=-1, keepdims=True)
     lanes = lax.broadcasted_iota(jnp.int32, (4, 128), 1)
     rows = lax.broadcasted_iota(jnp.int32, (4, 128), 0)
     near = gain_v[:, pl.ds(pl.multiple_of(128 * (group // 8), 128), 128)]
     at = lax.rem(group, 8) * 16 + dp * 4
     gains = jnp.sum(jnp.where(lanes == at + rows, jnp.broadcast_to(near, (4, 128)), 0.0), axis=-1, keepdims=True)
-    ratio = jnp.broadcast_to(summed / gains, (4, 128))
-    gain_out[...] = jnp.sum(jnp.where(lanes == rows, ratio, 0.0), axis=0, keepdims=True)
+    w_rows = w_rows / gains
+    take_all(fourth)
+    add_last()
+
+    summed = jnp.broadcast_to(jnp.sum(w_rows * qkv_out[...], axis=-1, keepdims=True), (4, 128))
+    gain_out[...] = jnp.sum(jnp.where(lanes == rows, summed, 0.0), axis=0, keepdims=True)
+    for copies in arriving + first + second + third + [fourth]:
+        for copy in copies:
+            copy.wait_send()
     wait_all(back)
 
 
@@ -488,6 +494,11 @@
     for copy in copies:
         copy.start()
     return copies
+
+
+def take_all(copies):
+    for copy in copies:
+        copy.wait_recv()
 
 
 def wait_all(copies):

time: 61.9 us -> 61.5 us (level)
  no operation moved by 1% of the time
where the time goes in v4:
time: 61.5 us; the launch traced here: 61.4 us
  Pallas kernels  60.7 us (99%)
  between operations  0.64 us (1%)
    pallas_call x1, Pallas kernels, core(): pl.pallas_call(core_kernel, out_shape=(block, block, jax.ShapeDtypeStruct...  58.1 us
    pallas_call x1, Pallas kernels, finish(): pl.pallas_call(finish_kernel, out_shape=tuple(shapes), in_specs=[any_spac...  2.67 us

profile of v4, /device:TPU:1, one launch (start us, length us, event | category | flops | bytes accessed | tf_op | source)
XLA Modules:
  0.0 61.4 jit_solution(481154851206768184)
XLA Ops:
  0.6 58.1 %window_attention.1 = (bf16[12,6,4,1024]{3,2,1,0:T(4,128)(2,1)}, bf16[12,6,4,1024]{3,2,1,0:T(4,128)(2,1)}, f32[4,1536]{1,0:T(4,128)}, f32[4,512]{1,0:T(4,128)}, f32[1,128]{1,0:T(1,128)}) custom-call(bf16[12,6,4,1024]{3,2,1,0:T(4,128)(2,1)} %bitcast.16, bf16[12,6,4,1024]{3,2,1,0:T(4,128)(2,1)} %bitcast.17, s32[6,4,12]{2,1,0:T(4,128)} %bitcast.18, ...), custom_call_target="tpu_custom_call" | custom-call | tf_op jit(solution)/shard_map/window_attention/pallas_call | solution.py:514
  58.7 2.7 %results.1 = (bf16[12,6,4,1024]{3,2,1,0:T(4,128)(2,1)}, bf16[12,6,4,1024]{3,2,1,0:T(4,128)(2,1)}, f32[4,1536]{1,0:T(4,128)}, f32[4,512]{1,0:T(4,128)}, f32[1,4]{1,0:T(1,128)}) custom-call(bf16[12,6,4,1024]{3,2,1,0:T(4,128)(2,1)} %get-tuple-element.15.refs_0_, bf16[12,6,4,1024]{3,2,1,0:T(4,128)(2,1)} %get-tuple-element.16.refs_1_, ...), custom_call_target="tpu_custom_call" | custom-call | tf_op jit(solution)/shard_map/results/pallas_call | solution.py:596

commit v5 on v4

--- a/solution.py
+++ b/solution.py
@@ -244,8 +244,8 @@
             )
         )
     ]
-    for copy in loads:
-        copy.start()
+    for n in (0, 1, 3):
+        loads[n].start()
 
     lat, lon, dp = place()
     y_hi, z = lat // 8, lax.rem(lat, 8)
@@ -277,6 +277,8 @@
             arriving[n].append(remote(block_part(src, sent[k]), window_part(dst, sent[k]), *sems, to[k]))
         local.append(pltpu.make_async_copy(block_part(src, own), window_part(dst, own), own_sem.at[n]))
         send_all(arriving[n] + local[n:])
+    for n in (2, 4, 5):
+        loads[n].start()
 
     @pl.when(odd == 1)
     def _():

time: 61.5 us -> 61.5 us (level)
  no operation moved by 1% of the time
where the time goes in v5:
time: 61.5 us; the launch traced here: 61.4 us
  Pallas kernels  60.7 us (99%)
  between operations  0.64 us (1%)
    pallas_call x1, Pallas kernels, core(): pl.pallas_call(core_kernel, out_shape=(block, block, jax.ShapeDtypeStruct...  58.1 us
    pallas_call x1, Pallas kernels, finish(): pl.pallas_call(finish_kernel, out_shape=tuple(shapes), in_specs=[any_spac...  2.67 us

profile of v5, /device:TPU:1, one launch (start us, length us, event | category | flops | bytes accessed | tf_op | source)
XLA Modules:
  0.0 61.4 jit_solution(13202046074762168973)
XLA Ops:
  0.6 58.1 %window_attention.1 = (bf16[12,6,4,1024]{3,2,1,0:T(4,128)(2,1)}, bf16[12,6,4,1024]{3,2,1,0:T(4,128)(2,1)}, f32[4,1536]{1,0:T(4,128)}, f32[4,512]{1,0:T(4,128)}, f32[1,128]{1,0:T(1,128)}) custom-call(bf16[12,6,4,1024]{3,2,1,0:T(4,128)(2,1)} %bitcast.16, bf16[12,6,4,1024]{3,2,1,0:T(4,128)(2,1)} %bitcast.17, s32[6,4,12]{2,1,0:T(4,128)} %bitcast.18, ...), custom_call_target="tpu_custom_call" | custom-call | tf_op jit(solution)/shard_map/window_attention/pallas_call | solution.py:516
  58.7 2.7 %results.1 = (bf16[12,6,4,1024]{3,2,1,0:T(4,128)(2,1)}, bf16[12,6,4,1024]{3,2,1,0:T(4,128)(2,1)}, f32[4,1536]{1,0:T(4,128)}, f32[4,512]{1,0:T(4,128)}, f32[1,4]{1,0:T(1,128)}) custom-call(bf16[12,6,4,1024]{3,2,1,0:T(4,128)(2,1)} %get-tuple-element.15.refs_0_, bf16[12,6,4,1024]{3,2,1,0:T(4,128)(2,1)} %get-tuple-element.16.refs_1_, ...), custom_call_target="tpu_custom_call" | custom-call | tf_op jit(solution)/shard_map/results/pallas_call | solution.py:598

commit v6 on v4

--- a/solution.py
+++ b/solution.py
@@ -305,16 +305,16 @@
         normed[rows_of(level), :] = unit
         inv[rows_of(level), :] = jnp.broadcast_to(inv_std, (CELLS, 128))
         hid[rows_of(level), :] = (unit * gain).astype(BF16)
+    loads[4].wait()
+    qkv[...] = dot(hid[...], wqkv[...]).astype(BF16)
+    hid_t[...] = hid[...].T
     take_all(arriving[1])
     local[1].wait()
     spread(dyv, wide)
     for level in range(LEV):
         dys[rows_of(level), :] = load_level(wide, level).astype(BF16)
-    loads[4].wait()
-    qkv[...] = dot(hid[...], wqkv[...]).astype(BF16)
     loads[5].wait()
     datt[...] = dot_nt(dys[...], wproj[...]).astype(BF16)
-    hid_t[...] = hid[...].T
     dys_t[...] = dys[...].T
 
     def attend(h):

time: 61.5 us -> 61.3 us (level)
  no operation moved by 1% of the time
where the time goes in v6:
time: 61.3 us; the launch traced here: 61.2 us
  Pallas kernels  60.5 us (99%)
  between operations  0.64 us (1%)
    pallas_call x1, Pallas kernels, core(): pl.pallas_call(core_kernel, out_shape=(block, block, jax.ShapeDtypeStruct...  57.9 us
    pallas_call x1, Pallas kernels, finish(): pl.pallas_call(finish_kernel, out_shape=tuple(shapes), in_specs=[any_spac...  2.67 us

profile of v6, /device:TPU:1, one launch (start us, length us, event | category | flops | bytes accessed | tf_op | source)
XLA Modules:
  0.0 61.2 jit_solution(2155716446306587214)
XLA Ops:
  0.6 57.9 %window_attention.1 = (bf16[12,6,4,1024]{3,2,1,0:T(4,128)(2,1)}, bf16[12,6,4,1024]{3,2,1,0:T(4,128)(2,1)}, f32[4,1536]{1,0:T(4,128)}, f32[4,512]{1,0:T(4,128)}, f32[1,128]{1,0:T(1,128)}) custom-call(bf16[12,6,4,1024]{3,2,1,0:T(4,128)(2,1)} %bitcast.16, bf16[12,6,4,1024]{3,2,1,0:T(4,128)(2,1)} %bitcast.17, s32[6,4,12]{2,1,0:T(4,128)} %bitcast.18, ...), custom_call_target="tpu_custom_call" | custom-call | tf_op jit(solution)/shard_map/window_attention/pallas_call | solution.py:514
  58.5 2.7 %results.1 = (bf16[12,6,4,1024]{3,2,1,0:T(4,128)(2,1)}, bf16[12,6,4,1024]{3,2,1,0:T(4,128)(2,1)}, f32[4,1536]{1,0:T(4,128)}, f32[4,512]{1,0:T(4,128)}, f32[1,4]{1,0:T(1,128)}) custom-call(bf16[12,6,4,1024]{3,2,1,0:T(4,128)(2,1)} %get-tuple-element.15.refs_0_, bf16[12,6,4,1024]{3,2,1,0:T(4,128)(2,1)} %get-tuple-element.16.refs_1_, ...), custom_call_target="tpu_custom_call" | custom-call | tf_op jit(solution)/shard_map/results/pallas_call | solution.py:596
